TPU v7x, 32 devices: a whole 2x2x4 slice. The times are simulated.
32 devices in a mesh: dp: 8 (over z, x), head: 4 (over y, core).
Axes of the slice: x: 2, y: 2, z: 4, core: 2. Of those that a mesh axis runs over, the one named last changes fastest.
Arguments:
- tokens: bfloat16 [131072, 128], P(('dp', 'head')), may hold values from -6 to 6
- cotangent: bfloat16 [131072, 128], P(('dp', 'head')), may hold values from -6 to 6
- lengths: int32 [32, 8], P('dp'), may hold values from 1 to 1024, 4096 in all within a row
- qkv_master: float32 [128, 384], P('dp', 'head'), may hold values from -0.61871843 to 0.61871843
- out_master: float32 [128, 128], P(('dp', 'head')), may hold values from -3 to 3
- up_master: float32 [128, 512], P('dp', 'head'), may hold values from -1.14904852 to 1.14904852
- down_master: float32 [128, 512], P('dp', 'head'), may hold values from -0.5745243 to 0.5745243
- norm_master: float32 [128, 4], P(('dp', 'head')), may hold values from -1.2 to 2.8
- qkv_first: float32 [128, 384], P('dp', 'head'), may hold values from -0.0078125 to 0.0078125
- out_first: float32 [128, 128], P(('dp', 'head')), may hold values from -0.0078125 to 0.0078125
- up_first: float32 [128, 512], P('dp', 'head'), may hold values from -0.0078125 to 0.0078125
- down_first: float32 [128, 512], P('dp', 'head'), may hold values from -0.0078125 to 0.0078125
- norm_first: float32 [128, 4], P(('dp', 'head')), may hold values from -0.0078125 to 0.0078125
- qkv_second: float32 [128, 384], P('dp', 'head'), may hold values from 1.5853287e-07 to 2.536526e-06
- out_second: float32 [128, 128], P(('dp', 'head')), may hold values from 1.5853287e-07 to 2.536526e-06
- up_second: float32 [128, 512], P('dp', 'head'), may hold values from 1.5853287e-07 to 2.536526e-06
- down_second: float32 [128, 512], P('dp', 'head'), may hold values from 1.5853287e-07 to 2.536526e-06
- norm_second: float32 [128, 4], P(('dp', 'head')), may hold values from 1.5853287e-07 to 2.536526e-06
Outputs:
- mixed: bfloat16 [131072, 128], P(('dp', 'head'))
- input_grad: bfloat16 [131072, 128], P(('dp', 'head'))
- grad_norm: float32 [], replicated
- qkv_new: float32 [128, 384], P('dp', 'head')
- qkv_first_new: float32 [128, 384], P('dp', 'head')
- qkv_second_new: float32 [128, 384], P('dp', 'head')
- out_new: float32 [128, 128], P(('dp', 'head'))
- out_first_new: float32 [128, 128], P(('dp', 'head'))
- out_second_new: float32 [128, 128], P(('dp', 'head'))
- up_new: float32 [128, 512], P('dp', 'head')
- up_first_new: float32 [128, 512], P('dp', 'head')
- up_second_new: float32 [128, 512], P('dp', 'head')
- down_new: float32 [128, 512], P('dp', 'head')
- down_first_new: float32 [128, 512], P('dp', 'head')
- down_second_new: float32 [128, 512], P('dp', 'head')
- norm_new: float32 [128, 4], P(('dp', 'head'))
- norm_first_new: float32 [128, 4], P(('dp', 'head'))
- norm_second_new: float32 [128, 4], P(('dp', 'head'))
- qkv_grad: float32 [128, 384], P('dp', 'head')
- out_grad: float32 [128, 128], P(('dp', 'head'))
- up_grad: float32 [128, 512], P('dp', 'head')
- down_grad: float32 [128, 512], P('dp', 'head')
- norm_grad: float32 [128, 4], P(('dp', 'head'))
- qkv_copy: bfloat16 [128, 384], P('dp', 'head')
- out_copy: bfloat16 [128, 128], P(('dp', 'head'))
- up_copy: bfloat16 [128, 512], P('dp', 'head')
- down_copy: bfloat16 [128, 512], P('dp', 'head')
- norm_copy: bfloat16 [128, 4], P(('dp', 'head'))
Inputs may be any that keep to these rules, and one draw needn't show every extreme that they name: `lengths`: each packed row holds 8 whole windows that fill it; the longest is 1024 tokens.
All inputs are finite; a program needn't handle non-finite values.
Results may differ from a plain program's by a relative error of at most 0.023.
Values may be sent and summed in bfloat16 or wider, within the bound.
A program may use at most 192 MiB of HBM per device.

v0:
```python
import jax
import jax.numpy as jnp
from jax import lax
from jax.sharding import PartitionSpec as P

ROW_LEN = 4096
MAX_LEN = 1024
BLOCK = 512
STEP = 5


NORM_EPS = 1e-05
CLIP_NORM = 0.25
BETA_ONE = 0.5
BETA_TWO = 0.5
ADAM_EPS = 1e-08
DECAY = 0.1
MASKED = -1e30


def layer_stats(value):
    mean = jnp.mean(value, axis=-1, keepdims=True)
    centred = value - mean
    spread = jnp.mean(centred * centred, axis=-1, keepdims=True)
    scale = lax.rsqrt(spread + NORM_EPS)
    return (centred * scale, scale)


def norm_back(grad, normed, scale, gain):
    scaled = grad * gain
    inner = jnp.mean(scaled, axis=-1, keepdims=True)
    along = jnp.mean(scaled * normed, axis=-1, keepdims=True)
    return scale * (scaled - inner - normed * along)


def segment_ids(lengths):
    ends = jnp.cumsum(lengths, axis=1)
    place = jnp.arange(ROW_LEN, dtype=jnp.int32)
    inside = jnp.sum((place[None, :, None] >= ends[:, None, :]).astype(jnp.int32), axis=2)
    offset = jnp.arange(lengths.shape[0], dtype=jnp.int32) * lengths.shape[1]
    return (inside + offset[:, None]).reshape(-1)


def gelu_exact(value):
    return jax.nn.gelu(value, approximate=False)


def contract(left, right, left_dim, right_dim):
    return lax.dot_general(
        left, right, (((left_dim,), (right_dim,)), ((), ())), preferred_element_type=jnp.float32
    )


def padded(value, fill):
    front = jnp.full((MAX_LEN,) + value.shape[1:], fill, value.dtype)
    return jnp.concatenate([front, value], axis=0)


def window(query, pad_keys, segment, pad_segment, start):
    span = MAX_LEN + BLOCK
    query_block = lax.dynamic_slice_in_dim(query, start, BLOCK, 0)
    key_block = lax.dynamic_slice_in_dim(pad_keys, start, span, 0)
    query_seg = lax.dynamic_slice_in_dim(segment, start, BLOCK, 0)
    key_seg = lax.dynamic_slice_in_dim(pad_segment, start, span, 0)
    query_place = start + jnp.arange(BLOCK, dtype=jnp.int32)
    key_place = start - MAX_LEN + jnp.arange(span, dtype=jnp.int32)
    allowed = (query_seg[:, None] == key_seg[None, :]) & (
        key_place[None, :] <= query_place[:, None]
    )
    raw = contract(query_block, key_block, 1, 1) * query.shape[1] ** (-0.5)
    return (query_block, key_block, jnp.where(allowed, raw, MASKED))


def fold_windows(pieces):
    blocks = pieces.shape[0]
    reach = MAX_LEN // BLOCK + 1
    width = pieces.shape[-1]
    split = pieces.reshape(blocks, reach, BLOCK, width)
    summed = jnp.zeros((blocks + reach - 1, BLOCK, width), jnp.float32)
    for offset in range(reach):
        summed = summed + jnp.pad(split[:, offset], ((offset, reach - 1 - offset), (0, 0), (0, 0)))
    return summed.reshape(-1, width)[MAX_LEN:]


def attend_forward(query, keys, values, segment):
    pad_keys = padded(keys, 0)
    pad_values = padded(values, 0)
    pad_segment = padded(segment, -1)

    def one(start):
        query_block, key_block, scores = window(query, pad_keys, segment, pad_segment, start)
        value_block = lax.dynamic_slice_in_dim(pad_values, start, MAX_LEN + BLOCK, 0)
        top = jnp.max(scores, axis=-1, keepdims=True)
        weights = jnp.exp(scores - top)
        total = jnp.sum(weights, axis=-1, keepdims=True)
        probs = (weights / total).astype(jnp.bfloat16)
        result = jnp.dot(probs, value_block, preferred_element_type=jnp.float32)
        return (result, (top + jnp.log(total))[:, 0])

    starts = jnp.arange(query.shape[0] // BLOCK, dtype=jnp.int32) * BLOCK
    result, log_total = lax.map(one, starts)
    return (result.reshape(query.shape), log_total.reshape(-1))


def attend_backward(query, keys, values, segment, log_total, grad_out):
    scale = query.shape[1] ** (-0.5)
    pad_keys = padded(keys, 0)
    pad_values = padded(values, 0)
    pad_segment = padded(segment, -1)

    def one(start):
        query_block, key_block, scores = window(query, pad_keys, segment, pad_segment, start)
        value_block = lax.dynamic_slice_in_dim(pad_values, start, MAX_LEN + BLOCK, 0)
        grad_block = lax.dynamic_slice_in_dim(grad_out, start, BLOCK, 0)
        total_block = lax.dynamic_slice_in_dim(log_total, start, BLOCK, 0)
        probs = jnp.exp(scores - total_block[:, None])
        prob_grad = contract(grad_block, value_block, 1, 1)
        inner = jnp.sum(probs * prob_grad, axis=-1, keepdims=True)
        score_grad = (probs * (prob_grad - inner)).astype(jnp.bfloat16)
        query_grad = jnp.dot(score_grad, key_block, preferred_element_type=jnp.float32) * scale
        key_grad = contract(score_grad, query_block, 0, 0) * scale
        value_grad = contract(probs.astype(jnp.bfloat16), grad_block, 0, 0)
        return (query_grad, key_grad, value_grad)

    starts = jnp.arange(query.shape[0] // BLOCK, dtype=jnp.int32) * BLOCK
    query_grad, key_grad, value_grad = lax.map(one, starts)
    return (query_grad.reshape(query.shape), fold_windows(key_grad), fold_windows(value_grad))


def adam(weight, first, second, grad, factor, rate, decay):
    clipped = grad * factor
    first_new = BETA_ONE * first + (1.0 - BETA_ONE) * clipped
    second_new = BETA_TWO * second + (1.0 - BETA_TWO) * clipped * clipped
    direction = (
        first_new
        / (1.0 - BETA_ONE**STEP)
        / (jnp.sqrt(second_new / (1.0 - BETA_TWO**STEP)) + ADAM_EPS)
    )
    return (weight - rate * (direction + decay * weight), first_new, second_new)


def per_device(
    tokens,
    cotangent,
    lengths,
    qkv_master,
    out_master,
    up_master,
    down_master,
    norm_master,
    qkv_first,
    out_first,
    up_first,
    down_first,
    norm_first,
    qkv_second,
    out_second,
    up_second,
    down_second,
    norm_second,
):
    head_size = qkv_master.shape[1] // 3
    w_qkv, w_up, w_down = (
        lax.all_gather(qkv_master.astype(jnp.bfloat16), "dp", axis=0, tiled=True),
        lax.all_gather(up_master.astype(jnp.bfloat16), "dp", axis=0, tiled=True),
        lax.all_gather(down_master.astype(jnp.bfloat16), "dp", axis=0, tiled=True),
    )
    w_out, norm_work = (
        lax.all_gather(out_master.astype(jnp.bfloat16), ("dp", "head"), axis=0, tiled=True),
        lax.all_gather(norm_master.astype(jnp.bfloat16), ("dp", "head"), axis=0, tiled=True),
    )
    gains = norm_work.astype(jnp.float32)
    segment = segment_ids(lengths)
    start_value = tokens.astype(jnp.float32)
    normed_one, scale_one = layer_stats(start_value)
    first = (normed_one * gains[:, 0] + gains[:, 1]).astype(jnp.bfloat16)
    rows_one = lax.all_gather(first, "head", axis=0, tiled=True)
    packed = jnp.dot(rows_one, w_qkv, preferred_element_type=jnp.float32).astype(jnp.bfloat16)
    query = packed[:, :head_size]
    keys = packed[:, head_size : 2 * head_size]
    values = packed[:, 2 * head_size :]
    attended, log_total = attend_forward(query, keys, values, segment)
    heads = lax.all_to_all(
        attended.astype(jnp.bfloat16), "head", split_axis=0, concat_axis=1, tiled=True
    )
    resid = start_value + jnp.dot(heads, w_out, preferred_element_type=jnp.float32)
    normed_two, scale_two = layer_stats(resid)
    second = (normed_two * gains[:, 2] + gains[:, 3]).astype(jnp.bfloat16)
    gelu_grad_of = lambda pre, incoming: jax.vjp(gelu_exact, pre)[1](incoming)[0]
    rows_two, grad_rows = (
        lax.all_gather(second, "head", axis=0, tiled=True),
        lax.all_gather(cotangent, "head", axis=0, tiled=True),
    )
    hidden_pre = jnp.dot(rows_two, w_up, preferred_element_type=jnp.float32)
    hidden = gelu_exact(hidden_pre).astype(jnp.bfloat16)
    part = hidden
    branch = lax.psum_scatter(
        contract(part, w_down, 1, 1).astype(jnp.bfloat16), "head", scatter_dimension=0, tiled=True
    ).astype(jnp.float32)
    mixed = (resid + branch).astype(jnp.bfloat16)
    down_grad = contract(grad_rows, hidden, 0, 0)
    hidden_grad = jnp.dot(grad_rows, w_down, preferred_element_type=jnp.float32)
    pre_grad = gelu_grad_of(hidden_pre, hidden_grad).astype(jnp.bfloat16)
    up_grad = contract(rows_two, pre_grad, 0, 0)
    part = pre_grad
    second_in = lax.psum_scatter(
        contract(part, w_up, 1, 1).astype(jnp.bfloat16), "head", scatter_dimension=0, tiled=True
    ).astype(jnp.float32)
    gain_two_grad = jnp.sum(second_in * normed_two, axis=0)
    shift_two_grad = jnp.sum(second_in, axis=0)
    resid_grad = cotangent.astype(jnp.float32) + norm_back(
        second_in, normed_two, scale_two, gains[:, 2]
    )
    resid_low = resid_grad.astype(jnp.bfloat16)
    out_grad = contract(heads, resid_low, 0, 0)
    heads_grad = contract(resid_low, w_out, 1, 1).astype(jnp.bfloat16)
    head_rows_grad = lax.all_to_all(heads_grad, "head", split_axis=1, concat_axis=0, tiled=True)
    query_grad, key_grad, value_grad = attend_backward(
        query, keys, values, segment, log_total, head_rows_grad
    )
    packed_grad = jnp.concatenate([query_grad, key_grad, value_grad], axis=1).astype(jnp.bfloat16)
    qkv_grad = contract(rows_one, packed_grad, 0, 0)
    part = packed_grad
    first_in = lax.psum_scatter(
        contract(part, w_qkv, 1, 1).astype(jnp.bfloat16), "head", scatter_dimension=0, tiled=True
    ).astype(jnp.float32)
    gain_one_grad = jnp.sum(first_in * normed_one, axis=0)
    shift_one_grad = jnp.sum(first_in, axis=0)
    input_grad = (resid_grad + norm_back(first_in, normed_one, scale_one, gains[:, 0])).astype(
        jnp.bfloat16
    )
    norm_grad = jnp.stack([gain_one_grad, shift_one_grad, gain_two_grad, shift_two_grad], axis=1)
    qkv_shard, up_shard, down_shard = (
        lax.psum_scatter(
            qkv_grad.astype(jnp.bfloat16), "dp", scatter_dimension=0, tiled=True
        ).astype(jnp.float32),
        lax.psum_scatter(
            up_grad.astype(jnp.bfloat16), "dp", scatter_dimension=0, tiled=True
        ).astype(jnp.float32),
        lax.psum_scatter(
            down_grad.astype(jnp.bfloat16), "dp", scatter_dimension=0, tiled=True
        ).astype(jnp.float32),
    )
    out_shard, norm_shard = (
        lax.psum_scatter(out_grad, ("dp", "head"), scatter_dimension=0, tiled=True),
        lax.psum_scatter(norm_grad, ("dp", "head"), scatter_dimension=0, tiled=True),
    )
    local_square = (
        jnp.sum(qkv_shard * qkv_shard)
        + jnp.sum(up_shard * up_shard)
        + jnp.sum(down_shard * down_shard)
        + jnp.sum(out_shard * out_shard)
        + jnp.sum(norm_shard * norm_shard)
    )
    total_square = lax.psum(local_square, ("dp", "head"))
    grad_norm = jnp.sqrt(total_square)
    factor = jnp.minimum(1.0, CLIP_NORM / grad_norm)
    qkv_new, qkv_first_new, qkv_second_new = adam(
        qkv_master, qkv_first, qkv_second, qkv_shard, factor, 0.1, DECAY
    )
    out_new, out_first_new, out_second_new = adam(
        out_master, out_first, out_second, out_shard, factor, 0.5, DECAY
    )
    up_new, up_first_new, up_second_new = adam(
        up_master, up_first, up_second, up_shard, factor, 0.1, DECAY
    )
    down_new, down_first_new, down_second_new = adam(
        down_master, down_first, down_second, down_shard, factor, 0.1, DECAY
    )
    norm_new, norm_first_new, norm_second_new = adam(
        norm_master, norm_first, norm_second, norm_shard, factor, 0.5, 0.0
    )
    return (
        mixed,
        input_grad,
        grad_norm,
        qkv_new,
        qkv_first_new,
        qkv_second_new,
        out_new,
        out_first_new,
        out_second_new,
        up_new,
        up_first_new,
        up_second_new,
        down_new,
        down_first_new,
        down_second_new,
        norm_new,
        norm_first_new,
        norm_second_new,
        qkv_shard,
        out_shard,
        up_shard,
        down_shard,
        norm_shard,
        qkv_new.astype(jnp.bfloat16),
        out_new.astype(jnp.bfloat16),
        up_new.astype(jnp.bfloat16),
        down_new.astype(jnp.bfloat16),
        norm_new.astype(jnp.bfloat16),
    )


def solution(mesh):
    return jax.shard_map(
        per_device,
        mesh=mesh,
        in_specs=(
            P(("dp", "head"), None),
            P(("dp", "head"), None),
            P("dp", None),
            P("dp", "head"),
            P(("dp", "head"), None),
            P("dp", "head"),
            P("dp", "head"),
            P(("dp", "head"), None),
            P("dp", "head"),
            P(("dp", "head"), None),
            P("dp", "head"),
            P("dp", "head"),
            P(("dp", "head"), None),
            P("dp", "head"),
            P(("dp", "head"), None),
            P("dp", "head"),
            P("dp", "head"),
            P(("dp", "head"), None),
        ),
        out_specs=(
            P(("dp", "head"), None),
            P(("dp", "head"), None),
            P(),
            P("dp", "head"),
            P("dp", "head"),
            P("dp", "head"),
            P(("dp", "head"), None),
            P(("dp", "head"), None),
            P(("dp", "head"), None),
            P("dp", "head"),
            P("dp", "head"),
            P("dp", "head"),
            P("dp", "head"),
            P("dp", "head"),
            P("dp", "head"),
            P(("dp", "head"), None),
            P(("dp", "head"), None),
            P(("dp", "head"), None),
            P("dp", "head"),
            P(("dp", "head"), None),
            P("dp", "head"),
            P("dp", "head"),
            P(("dp", "head"), None),
            P("dp", "head"),
            P(("dp", "head"), None),
            P("dp", "head"),
            P("dp", "head"),
            P(("dp", "head"), None),
        ),
        check_vma=False,
    )
```

profile of v0, /device:TPU:0, one launch (start us, length us, event | category | flops | bytes accessed | tf_op | source)
XLA Modules:
  0.0 1465.9 jit_solution(1877056919273896609)
XLA Ops:
  7.9 43.2 %all-gather = bf16[32,4,4]{2,1,0:T(4,128)(2,1)S(1)} all-gather(bf16[1,4,4]{2,1,0:T(4,128)(2,1)S(1)} %convert_bitcast_fusion.2), channel_id=1, replica_groups=mesh['dp'=8,'head'=4] {'dp','head'}, dimensions={0}, use_global_device_ids=true | all-gather | bytes 1056 | tf_op jit(solution)/shard_map/all_gather | solution.py:170
  56.1 30.4 %all_gather.26 = bf16[128,96]{1,0:T(8,128)(2,1)S(1)} all-gather(bf16[16,96]{1,0:T(8,128)(2,1)S(1)} %convert_element_type.148), channel_id=1, replica_groups=mesh['dp'=8,'head'=4] {'dp'}, dimensions={0}, use_global_device_ids=true | all-gather | bytes 27648 | tf_op jit(solution)/shard_map/all_gather | solution.py:164
  91.5 4.7 copy.206
  102.4 6.1 concatenate.18.clone
  108.5 3.8 concatenate.17.clone
  112.4 317.2 %while.30 = (s32[]{:T(128)}, bf16[32,512,32]{1,2,0:T(8,128)(2,1)S(1)}, f32[32,512]{1,0:T(8,128)S(1)}, s32[32]{0:T(128)S(1)}, s32[16384]{0:T(1024)S(1)}, /*index=...) while((s32[]{:T(128)}, ...), condition=%wide.region_7.8_spmd, body=%wide.region_4.7_spmd.sunk | while | flops 109315592 | bytes 10481924 | solution.py:101
  432.5 3.5 all-to-all-start
  436.3 46.0 %all-gather.1 = bf16[32,4,128]{2,1,0:T(4,128)(2,1)S(1)} all-gather(bf16[1,4,128]{2,1,0:T(4,128)(2,1)S(1)} %convert_bitcast_fusion.1), channel_id=1, replica_groups=mesh['dp'=8,'head'=4] {'dp','head'}, dimensions={0}, use_global_device_ids=true | all-gather | bytes 33792 | tf_op jit(solution)/shard_map/all_gather | solution.py:169
  487.5 30.4 %all_gather.30 = bf16[128,128]{1,0:T(8,128)(2,1)S(1)} all-gather(bf16[16,128]{1,0:T(8,128)(2,1)S(1)} %convert_element_type.156), channel_id=1, replica_groups=mesh['dp'=8,'head'=4] {'dp'}, dimensions={0}, use_global_device_ids=true | all-gather | bytes 36864 | tf_op jit(solution)/shard_map/all_gather | solution.py:166
  517.9 30.6 %all_gather.29 = bf16[128,128]{1,0:T(8,128)(2,1)S(1)} all-gather(bf16[16,128]{1,0:T(8,128)(2,1)S(1)} %convert_element_type.154), channel_id=1, replica_groups=mesh['dp'=8,'head'=4] {'dp'}, dimensions={0}, use_global_device_ids=true | all-gather | bytes 36864 | tf_op jit(solution)/shard_map/all_gather | solution.py:165
  548.5 6.7 fusion.92
  555.2 22.8 %add_convert_fusion = (bf16[16384,128]{1,0:T(8,128)(2,1)S(1)}, f32[16384,128]{1,0:T(8,128)}) fusion(f32[16384,128]{1,0:T(8,128)} %fusion.92, bf16[16384,128]{1,0:T(8,128)(2,1)} %all-gather.10.cloned.1.call-done, bf16[128,128]{1,0:T(8,128)(2,1)S(1)} %all_gather.30), kind=kOutput, calls=%fused_computation.52 | convolution fusion | flops 687865856 | bytes 25198592 | tf_op jit(solution)/shard_map/dot_general | solution.py:202
  580.1 3.3 convolution_convert_fusion.1
  583.4 7.4 multiply_convert_fusion.1
  598.5 6.0 convolution_convert_fusion.6
  604.6 21.7 %reduce-scatter.10.cloned.1.call-done = bf16[4096,128]{0,1:T(8,128)(2,1)} async-done(((bf16[16384,128]{0,1:T(8,128)(2,1)}), bf16[4096,128]{0,1:T(8,128)(2,1)}) %reduce-scatter.10.cloned.1.call-update) | async-done | bytes 1048592 | tf_op jit(solution)/shard_map/reduce_scatter | solution.py:206
  628.5 44.9 %reduce-scatter.8.cloned.1.call-done = bf16[4096,128]{0,1:T(8,128)(2,1)} async-done(((bf16[16384,128]{0,1:T(8,128)(2,1)}), bf16[4096,128]{0,1:T(8,128)(2,1)}) %reduce-scatter.8.cloned.1.call-update) | async-done | bytes 1048592 | tf_op jit(solution)/shard_map/reduce_scatter | solution.py:197
  673.4 3.4 fusion.58
  679.5 4.5 all-to-all-start.1
  684.0 5.6 fusion.64
  690.8 7.7 all-to-all-done.1
  698.5 4.6 copy.165
  703.2 495.9 %while.31 = (s32[]{:T(128)}, bf16[32,512,32]{1,2,0:T(8,128)(2,1)S(1)}, f32[32,1536,32]{1,2,0:T(8,128)}, f32[32,1536,32]{1,2,0:T(8,128)}, s32[32]{0:T(128)S(1)}, ...) while((s32[]{:T(128)}, ...), condition=%wide.region_16.17_spmd, body=%wide.region_14.16_spmd.sunk | while | flops 261162496 | bytes 25807156 | solution.py:126
  1200.2 11.4 reshape.193
  1211.6 14.3 fusion.87
  1227.6 11.4 reshape.192
  1239.0 14.2 fusion.88
  1259.7 5.1 convolution_convert_fusion
  1269.6 43.7 %reduce-scatter.14.cloned.1.call-done = bf16[16,96]{1,0:T(8,128)(2,1)} async-done(((bf16[128,96]{1,0:T(8,128)(2,1)}), bf16[16,96]{1,0:T(8,128)(2,1)}) %reduce-scatter.14.cloned.1.call-update) | async-done | bytes 3088 | tf_op jit(solution)/shard_map/reduce_scatter | solution.py:234
  1317.2 42.1 %reduce-scatter.12.cloned.1.call-done = bf16[4096,128]{0,1:T(8,128)(2,1)} async-done(((bf16[16384,128]{0,1:T(8,128)(2,1)}), bf16[4096,128]{0,1:T(8,128)(2,1)}) %reduce-scatter.12.cloned.1.call-update) | async-done | bytes 1048592 | tf_op jit(solution)/shard_map/reduce_scatter | solution.py:224
  1361.5 39.3 %all-reduce.10 = f32[128,4]{0,1:T(4,128)S(1)} all-reduce(f32[128,4]{0,1:T(4,128)S(1)} %pad_maximum_fusion), channel_id=9, replica_groups=mesh['dp'=8,'head'=4] {'dp','head'}, use_global_device_ids=true, to_apply=%region_32.33.clone | all-reduce | flops 512 | bytes 4096
  1404.4 40.9 %psum.7 = f32[]{:T(128)} all-reduce(f32[]{:T(128)S(6)} %add.330), channel_id=1, replica_groups=mesh['dp'=8,'head'=4] {'dp','head'}, use_global_device_ids=true, to_apply=%region_34.35 | all-reduce | flops 1 | bytes 8 | tf_op jit(solution)/shard_map/psum | solution.py:255
  (910 shorter events, 635.2 us)
Async XLA Ops:
  7.2 79.3 %all-gather.6.cloned.1.call-start = ((), (), s32[]{:S(2)}) async-start(), calls=%async_computation.8 | async-start | bytes 5242880 | tf_op jit(solution)/shard_map/all_gather | solution.py:177
  52.9 430.3 %copy-start = (bf16[4096,128]{0,1:T(8,128)(2,1)}, bf16[4096,128]{0,1:T(8,128)(2,1)S(1)}, u32[]{:S(2)}) copy-start(bf16[4096,128]{0,1:T(8,128)(2,1)S(1)} %copy.152) | copy-start | bytes 3145732
  102.4 6.1 copy-start.9
  430.2 6.1 copy-start.36
  432.5 49.7 %all-to-all-start = ((bf16[4,4096,32]{1,2,0:T(8,128)(2,1)}), bf16[4,4096,32]{1,2,0:T(8,128)(2,1)S(1)}, u32[]{:S(2)}, u32[]{:S(2)}) async-start(bf16[4,4096,32]{1,2,0:T(8,128)(2,1)} %copy.159), calls=%async_computation | async-start | bytes 2097152 | tf_op jit(solution)/shard_map/all_to_all | solution.py:183
  436.1 112.4 %all-gather.8.cloned.1.call-start = ((), (), s32[]{:S(2)}) async-start(), calls=%async_computation.9 | async-start | bytes 5242880 | tf_op jit(solution)/shard_map/all_gather | solution.py:191
  486.6 68.5 %all-gather.10.cloned.1.call-start = ((), (), s32[]{:S(2)}) async-start(), calls=%async_computation.11 | async-start | bytes 5242880 | tf_op jit(solution)/shard_map/all_gather | solution.py:192
  487.4 138.9 %reduce-scatter.10.cloned.1.call-start = ((), (), s32[]{:S(2)}) async-start(), calls=%async_computation.12 | async-start | bytes 5242880 | tf_op jit(solution)/shard_map/reduce_scatter | solution.py:206
  583.3 90.0 %reduce-scatter.8.cloned.1.call-start = ((), (), s32[]{:S(2)}) async-start(), calls=%async_computation.10 | async-start | bytes 5242880 | tf_op jit(solution)/shard_map/reduce_scatter | solution.py:197
  596.0 669.7 %reduce-scatter.16.cloned.1.call-start = ((), (), s32[]{:S(2)}) async-start(), calls=%async_computation.15 | async-start | bytes 36864 | tf_op jit(solution)/shard_map/reduce_scatter | solution.py:237
  626.2 47.1 %copy-start.12 = (bf16[4096,128]{0,1:T(8,128)(2,1)S(1)}, bf16[4096,128]{0,1:T(8,128)(2,1)}, u32[]{:S(2)}) copy-start(bf16[4096,128]{0,1:T(8,128)(2,1)} %reduce-scatter.10.cloned.1.call-done) | copy-start | bytes 3145732
  679.5 19.0 %all-to-all-start.1 = ((bf16[4096,4,32]{0,2,1:T(8,128)(2,1)}), bf16[4096,4,32]{0,2,1:T(8,128)(2,1)}, u32[]{:S(2)}, u32[]{:S(2)}) async-start(bf16[4096,4,32]{0,2,1:T(8,128)(2,1)} %bitcast.18), calls=%async_computation.3 | async-start | bytes 2097152 | tf_op jit(solution)/shard_map/all_to_all | solution.py:217
  684.0 583.0 %reduce-scatter.18.cloned.1.call-start = ((), (), s32[]{:S(2)}) async-start(), calls=%async_computation.16 | async-start | bytes 36864 | tf_op jit(solution)/shard_map/reduce_scatter | solution.py:240
  689.6 578.7 %all-reduce.13.cloned.1.call-start = ((), (), s32[]{:S(2)}) async-start(), calls=%async_computation.17 | async-start | bytes 131072
  690.8 622.5 %reduce-scatter.14.cloned.1.call-start = ((), (), s32[]{:S(2)}) async-start(), calls=%async_computation.14 | async-start | bytes 36864 | tf_op jit(solution)/shard_map/reduce_scatter | solution.py:234
  1259.6 99.7 %reduce-scatter.12.cloned.1.call-start = ((), (), s32[]{:S(2)}) async-start(), calls=%async_computation.13 | async-start | bytes 5242880 | tf_op jit(solution)/shard_map/reduce_scatter | solution.py:224
  1264.8 94.5 %copy-start.1 = (bf16[4096,128]{0,1:T(8,128)(2,1)S(1)}, bf16[4096,128]{0,1:T(8,128)(2,1)}, u32[]{:S(2)}) copy-start(bf16[4096,128]{0,1:T(8,128)(2,1)} %copy-done) | copy-start | bytes 3145732
  1264.8 94.5 %copy-start.15 = (f32[4096]{0:T(1024)S(1)}, f32[4096]{0:T(1024)}, u32[]{:S(2)}) copy-start(f32[4096]{0:T(1024)} %copy-done.14) | copy-start | bytes 49156
  1264.8 94.5 %copy-start.19 = (f32[4096]{0:T(1024)S(1)}, f32[4096]{0:T(1024)}, u32[]{:S(2)}) copy-start(f32[4096]{0:T(1024)} %copy-done.18) | copy-start | bytes 49156
  1264.8 94.5 %copy-start.40 = (f32[128,1]{0,1:T(1,128)S(1)}, f32[128,1]{0,1:T(1,128)}, u32[]{:S(2)}) copy-start(f32[128,1]{0,1:T(1,128)} %copy-done.39) | copy-start | bytes 1540
  1267.0 189.1 %copy-start.26 = (f32[16,128]{1,0:T(8,128)}, f32[16,128]{1,0:T(8,128)S(1)}, u32[]{:S(2)}) copy-start(f32[16,128]{1,0:T(8,128)S(1)} %get-tuple-element.571) | copy-start | bytes 24580
  1268.3 187.2 %copy-start.27 = (f32[16,128]{1,0:T(8,128)}, f32[16,128]{1,0:T(8,128)S(1)}, u32[]{:S(2)}) copy-start(f32[16,128]{1,0:T(8,128)S(1)} %get-tuple-element.569) | copy-start | bytes 24580
  1269.6 185.3 %copy-start.38 = (f32[4,128]{1,0:T(4,128)}, f32[4,128]{1,0:T(4,128)S(1)}, u32[]{:S(2)}) copy-start(f32[4,128]{1,0:T(4,128)S(1)} %get-tuple-element.567) | copy-start | bytes 6148
  1314.6 142.2 %copy-start.28 = (f32[16,96]{1,0:T(8,128)}, f32[16,96]{1,0:T(8,128)S(1)}, u32[]{:S(2)}) copy-start(f32[16,96]{1,0:T(8,128)S(1)} %get-tuple-element.573) | copy-start | bytes 18436
  1449.5 6.0 copy-start.21
  1449.5 6.0 copy-start.29
  1449.5 6.6 copy-start.23
  1449.6 6.6 copy-start.31
  1449.6 6.6 copy-start.32
  1449.6 7.2 copy-start.25
  1449.6 7.2 copy-start.33
  1449.6 7.2 copy-start.34
  (26 other events, 67.7 us)
Sparse Core Ops, SparseCore 0:
  55.6 30.5 all-gather.5
  486.8 30.5 all-gather.7
  518.9 34.4 all-gather.9
  583.5 42.7 reduce-scatter.9
  628.8 44.5 reduce-scatter.7
  676.3 53.5 reduce-scatter.15
  733.1 52.6 reduce-scatter.17
  791.9 116.7 all-reduce.12
  1259.7 53.5 reduce-scatter.13
  1315.7 43.5 reduce-scatter.11
where the time goes:
time: 1490 us; the launch traced here: 1470 us
  matrix products  501 us (34%)
  blocking collectives  261 us (18%)
  loops' own time  251 us (17%)
  waiting for transfers between devices  161 us (11%)
  local copies, waits for them, and re-layouts  159 us (11%)
  other arithmetic  104 us (7%)
  between operations  20.5 us (1%)
    dot_general x168, matrix products, contract(): lax.dot_general(left, right, (((left_dim,), (right_dim,)), ((), ())), pre...  357 us
    another operation x1, loops' own time, attend_forward(): result, log_total = lax.map(one, starts)  126 us
    another operation x1, loops' own time, attend_backward(): query_grad, key_grad, value_grad = lax.map(one, starts)  125 us
    dot_general x32, matrix products, one(): result = jnp.dot(probs, value_block, preferred_element_type=jnp.float32)  59.7 us
    dot_general x32, matrix products, one(): jnp.dot(score_grad, key_block, preferred_element_type=jnp.float32) * scale  50.1 us
    all_gather x1, blocking collectives, per_device(): lax.all_gather(out_master.astype(jnp.bfloat16), ('dp', 'head'), axis=0, t...  46 us
    reduce_scatter x1, waiting for transfers between devices, per_device(): lax.psum_scatter(contract(part, w_down, 1, 1).astype(jnp.bfloat16), 'head...  44.9 us
    reduce_scatter x1, waiting for transfers between devices, per_device(): lax.psum_scatter(qkv_grad.astype(jnp.bfloat16), 'dp', scatter_dimension=0...  43.7 us
  transfers between devices with their start and end apart: 12, of which 5 were waited for; matrix products, arithmetic and copies ran while one was open for 33% of the time, Pallas kernels for 0%

commit v1 on v0

v1 whole, which is shorter than its diff:
```python
import functools
import math

import jax
import jax.numpy as jnp
from jax import lax
from jax.experimental import pallas as pl
from jax.experimental.pallas import tpu as pltpu
from jax.sharding import PartitionSpec as P

MAX_LEN = 1024
STEP = 5
NORM_EPS = 1e-05
CLIP_NORM = 0.25
BETA_ONE = 0.5
BETA_TWO = 0.5
ADAM_EPS = 1e-08
DECAY = 0.1
HEADS = 4
HD = 32
D = 128
FF = 512
B = 256
CAP = 50
BIG = 2.0**100
LIMIT = 88.0
MASKED = -1e30
LN2 = math.log(2.0)
QSCALE = HD**-0.5 / LN2
f32 = jnp.float32
bf16 = jnp.bfloat16
MESH = pl.DeviceIdType.MESH


def mm(a, b):
    return lax.dot_general(a, b, (((1,), (0,)), ((), ())), preferred_element_type=f32)


def mm_nt(a, b):
    return lax.dot_general(a, b, (((1,), (1,)), ((), ())), preferred_element_type=f32)


def stats(value):
    mean = jnp.mean(value, axis=0, keepdims=True)
    centred = value - mean
    spread = jnp.mean(centred * centred, axis=0, keepdims=True)
    rate = lax.rsqrt(spread + NORM_EPS)
    return centred * rate, rate


def norm_back(grad, normed, rate, gain):
    scaled = grad * gain
    inner = jnp.mean(scaled, axis=0, keepdims=True)
    along = jnp.mean(scaled * normed, axis=0, keepdims=True)
    return rate * (scaled - inner - normed * along)


def split3(value):
    one = value.astype(bf16).astype(f32)
    two = (value - one).astype(bf16).astype(f32)
    return one, two, value - one - two


def lane_fold(value):
    out = value[:, :128]
    for j in range(1, value.shape[1] // 128):
        out = out + value[:, j * 128 : (j + 1) * 128]
    return out


def layer_kernel(
    rd,
    ro,
    lengths,
    w_ref,
    tokens,
    cot,
    mixed,
    igrad,
    grads,
    uq,
    uk,
    us,
    bounds,
    wqkv_t,
    wqkv,
    wout,
    wout_t,
    wup,
    wup_t,
    wdown,
    wdown_t,
    gains,
    stage,
    qf,
    kf,
    vf,
    kt,
    vt,
    dof,
    probs,
    ds,
    acc,
    dk_acc,
    dv_acc,
    resid_grad,
    first,
    causal,
    qn,
    kn,
    g_qkv,
    g_out,
    g_up,
    g_down,
    g_norm,
    g_stage,
):
    n_head, n_dp = w_ref.shape[:2]
    tiles = tokens.shape[0] // B
    row = lax.rem(lax.axis_index("head"), n_head)

    for h in range(n_head):
        qkv_h = jnp.concatenate([w_ref[h, d].astype(f32) for d in range(n_dp)], axis=0)
        stage[...] = qkv_h
        rp = w_ref.shape[2]
        pick = lambda lo, n: jnp.concatenate(
            [stage[d * rp + lo : d * rp + lo + n] for d in range(n_dp)], axis=0
        )
        q = pick(0, rd)
        wqkv_t[h] = q.T[: 3 * HD].astype(bf16)
        wqkv[:, h * 128 : (h + 1) * 128] = q.astype(bf16)
        u = pick(rd, rd)
        wup[:, h * 128 : (h + 1) * 128] = u.astype(bf16)
        wup_t[h * 128 : (h + 1) * 128] = u.T.astype(bf16)
        u = pick(2 * rd, rd)
        wdown[:, h * 128 : (h + 1) * 128] = u.astype(bf16)
        wdown_t[h * 128 : (h + 1) * 128] = u.T.astype(bf16)
        for d in range(n_dp):
            at = (d * n_head + h) * ro
            g_out[at : at + ro] = stage[d * rp + 3 * rd : d * rp + 3 * rd + ro]
            gains[at : at + ro] = stage[d * rp + 3 * rd + ro : d * rp + 3 * rd + 2 * ro]
    wo = g_out[...]
    wout[...] = wo.astype(bf16)
    wout_t[...] = wo.T.astype(bf16)
    gain1, shift1 = gains[:, 0:1], gains[:, 1:2]
    gain2, shift2 = gains[:, 2:3], gains[:, 3:4]

    starts, ends = [], []
    at = jnp.int32(0)
    for s in range(lengths.shape[1]):
        starts.append(at)
        at = at + lengths[row, s]
        ends.append(at)
    place = lax.broadcasted_iota(jnp.int32, (8, B), 0)
    start_v = jnp.zeros((8, B), jnp.int32)
    end_v = jnp.zeros((8, B), jnp.int32)
    for s in range(8):
        start_v = jnp.where(place == s, starts[s], start_v)
        end_v = jnp.where(place == s, ends[s], end_v)
    uq[0] = 0
    uk[0] = 0
    us[0] = 0

    def list_q(i, n):
        low = jnp.int32(0)
        for s in range(1, 8):
            low = jnp.where(starts[s] <= i * B, starts[s], low)

        def list_k(j, n):
            uq[n] = i
            uk[n] = j
            us[n] = jnp.minimum(n, CAP + 1)
            return n + 1

        return lax.fori_loop(lax.div(low, B), i + 1, list_k, n)

    units = lax.fori_loop(0, tiles, list_q, jnp.int32(1))
    uq[units] = 0
    uk[units] = 0
    us[units] = 0

    key_i = lax.broadcasted_iota(jnp.int32, (B, B), 0)
    query_i = lax.broadcasted_iota(jnp.int32, (B, B), 1)
    allowed = key_i <= query_i
    causal[0] = jnp.full((B, B), jnp.inf, bf16)
    causal[1] = jnp.where(allowed, jnp.inf, 0.0).astype(bf16)
    probs[0] = jnp.zeros_like(probs[0])
    ds[...] = jnp.zeros_like(ds)
    qn[...] = jnp.zeros_like(qn)
    kn[...] = jnp.zeros_like(kn)
    for ref in (acc, dk_acc, dv_acc, g_qkv, g_out, g_up, g_down, g_norm):
        ref[...] = jnp.zeros_like(ref)

    def project(i, carry):
        x = tokens[pl.ds(pl.multiple_of(i * B, B), B), :].astype(f32).T
        n1, _ = stats(x)
        f = (n1 * gain1 + shift1).astype(bf16)
        first[i] = f
        where_t = i * B + lax.broadcasted_iota(jnp.int32, (8, B), 1)
        inside = ((where_t >= start_v) & (where_t < end_v)).astype(f32)
        penalty = (1.0 - inside) * -BIG
        zeros8 = jnp.zeros((8, B), f32)
        ones8 = jnp.ones((8, B), f32)
        zeros16 = jnp.zeros((16, B), f32)
        for h in range(HEADS):
            packed = mm(wqkv_t[h], f).astype(bf16)
            pf = packed.astype(f32)
            q = (pf[:HD] * QSCALE).astype(bf16).astype(f32)
            k = pf[HD : 2 * HD]
            v = pf[2 * HD :]
            qn[h] = jnp.maximum(qn[h], jnp.sum(q * q, axis=0, keepdims=True))
            kn[h] = jnp.maximum(kn[h], jnp.sum(k * k, axis=0, keepdims=True))
            qf[h, i] = jnp.concatenate([q, penalty, zeros8, zeros16], axis=0).astype(bf16)
            kf[h, i] = packed[HD : 2 * HD]
            vf[h, i] = jnp.concatenate([v, ones8, zeros8], axis=0).astype(bf16)
            kt[h, i] = jnp.concatenate([k, inside, ones8, zeros16], axis=0).T.astype(bf16)
            vt[h, i] = jnp.concatenate([v, ones8, zeros8, zeros16], axis=0).T.astype(bf16)
        return carry

    lax.fori_loop(0, tiles, project, 0)

    bound = jnp.float32(0.0)
    for h in range(HEADS):
        bound = jnp.maximum(bound, jnp.max(qn[h]) * jnp.max(kn[h]))

    def scores(h, i, j):
        return mm(kt[h, j], qf[h, i])

    @pl.when(jnp.logical_not(bound <= LIMIT * LIMIT))
    def _():
        bounds[...] = jnp.full_like(bounds, MASKED)

        def top(t, carry):
            i, j = uq[t], uk[t]
            masked = jnp.where(allowed | (i != j), 0.0, MASKED)
            for h in range(HEADS):
                s = scores(h, i, j) + masked
                bounds[h, i] = jnp.maximum(bounds[h, i], jnp.max(s, axis=0, keepdims=True))
            return carry

        lax.fori_loop(1, units, top, 0)

        def shift(i, carry):
            for h in range(HEADS):
                one, two, three = split3(-bounds[h, i])
                r = lax.broadcasted_iota(jnp.int32, (16, B), 0)
                old = qf[h, i, HD : HD + 16].astype(f32)
                new = jnp.where(r == 8, one, jnp.where(r == 9, two, jnp.where(r == 10, three, old)))
                qf[h, i, HD : HD + 16] = new.astype(bf16)
            return carry

        lax.fori_loop(0, tiles, shift, 0)

    def weigh(t, slot):
        i, j = uq[t], uk[t]
        cut = causal[jnp.where(i == j, 1, 0)]
        for h in range(HEADS):
            probs[slot, h] = jnp.minimum(jnp.exp2(scores(h, i, j)).astype(bf16), cut)

    def forward(t, carry):
        i, j, slot = uq[t - 1], uk[t - 1], jnp.minimum(t - 1, CAP + 1)
        for h in range(HEADS):
            acc[h, i] += mm(vf[h, j, : HD + 8], probs[slot, h])
        weigh(t, jnp.minimum(t, CAP + 1))
        return carry

    lax.fori_loop(1, units + 1, forward, 0)

    def feed(i, carry):
        at = pl.ds(pl.multiple_of(i * B, B), B)
        outs, inv = [], []
        for h in range(HEADS):
            r = 1.0 / acc[h, i, HD : HD + 1]
            inv.append(r)
            outs.append(acc[h, i, :HD] * r)
        heads = jnp.concatenate(outs, axis=0).astype(bf16)
        x = tokens[at, :].astype(f32).T
        resid = x + mm(wout_t[...], heads)
        n2, rate2 = stats(resid)
        second = (n2 * gain2 + shift2).astype(bf16)
        c32 = cot[at, :].astype(f32).T
        c16 = c32.astype(bf16)
        pre = mm(wup_t[...], second)
        back = mm(wdown_t[...], c16)
        cdf = 0.5 * (1.0 + lax.erf(pre * (0.5**0.5)))
        pdf = jnp.exp(-0.5 * pre * pre) * (1.0 / math.sqrt(2.0 * math.pi))
        hidden = (pre * cdf).astype(bf16)
        pre_grad = (back * (cdf + pre * pdf)).astype(bf16)
        mixed[at, :] = (resid + mm(wdown[...], hidden)).T.astype(bf16)
        g_down[...] += mm_nt(c16, hidden)
        g_up[...] += mm_nt(second, pre_grad)
        second_in = mm(wup[...], pre_grad)
        g_norm[2] += lane_fold(second_in * n2)
        g_norm[3] += lane_fold(second_in)
        rg = c32 + norm_back(second_in, n2, rate2, gain2)
        resid_grad[i] = rg
        low = rg.astype(bf16)
        g_out[...] += mm_nt(heads, low)
        hg = mm(wout[...], low).astype(bf16).astype(f32)
        zeros16 = jnp.zeros((16, B), f32)
        r8 = lax.broadcasted_iota(jnp.int32, (16, B), 0)
        for h in range(HEADS):
            do = (hg[h * HD : (h + 1) * HD] * inv[h]).astype(bf16).astype(f32)
            delta = jnp.sum(do * outs[h], axis=0, keepdims=True)
            one, two, three = split3(-delta)
            extra = jnp.where(r8 == 0, one, jnp.where(r8 == 1, two, jnp.where(r8 == 2, three, 0.0)))
            dof[h, i] = jnp.concatenate([do, extra, zeros16], axis=0).astype(bf16)
        return carry

    lax.fori_loop(0, tiles, feed, 0)
    acc[...] = jnp.zeros_like(acc)

    def backward(t, carry):
        i, j = uq[t - 1], uk[t - 1]
        old = lax.rem(t - 1, 2)
        for h in range(HEADS):
            sg = ds[old, h]
            acc[h, i, :HD] += mm(kf[h, j], sg)
            dk_acc[h, j] += mm_nt(qf[h, i, :HD], sg)
        i, j, slot = uq[t], uk[t], us[t]
        pl.when(slot > CAP)(lambda: weigh(t, slot))
        new = lax.rem(t, 2)
        for h in range(HEADS):
            p = probs[slot, h]
            pg = mm(vt[h, j], dof[h, i])
            ds[new, h] = (p.astype(f32) * pg).astype(bf16)
            dv_acc[h, j] += mm_nt(dof[h, i, :HD], p)
        return carry

    lax.fori_loop(1, units + 1, backward, 0)

    def finish(i, carry):
        at = pl.ds(pl.multiple_of(i * B, B), B)
        rows = []
        for h in range(HEADS):
            rows += [acc[h, i, :HD] * HD**-0.5, dk_acc[h, i] * LN2, dv_acc[h, i], jnp.zeros((HD, B), f32)]
        packed_grad = jnp.concatenate(rows, axis=0).astype(bf16)
        g_qkv[...] += mm_nt(first[i], packed_grad)
        first_in = mm(wqkv[...], packed_grad)
        x = tokens[at, :].astype(f32).T
        n1, rate1 = stats(x)
        g_norm[0] += lane_fold(first_in * n1)
        g_norm[1] += lane_fold(first_in)
        out = resid_grad[i] + norm_back(first_in, n1, rate1, gain1)
        igrad[at, :] = out.T.astype(bf16)
        return carry

    lax.fori_loop(0, tiles, finish, 0)

    lane = lax.broadcasted_iota(jnp.int32, (D, 128), 1)
    norm = jnp.zeros((D, 128), f32)
    for c in range(4):
        norm = jnp.where(lane == c, jnp.sum(g_norm[c], axis=1, keepdims=True), norm)
    gains[...] = norm
    g_stage[...] = jnp.zeros_like(g_stage)
    for h in range(n_head):
        cols = slice(h * 128, (h + 1) * 128)
        for d in range(n_dp):
            rows = slice(d * rd, (d + 1) * rd)
            at = (d * n_head + h) * ro
            g_stage[0:rd] = g_qkv[rows, cols]
            g_stage[rd : 2 * rd] = g_up[rows, cols]
            g_stage[2 * rd : 3 * rd] = g_down[rows, cols]
            g_stage[3 * rd : 3 * rd + ro] = g_out[at : at + ro]
            g_stage[3 * rd + ro : 3 * rd + 2 * ro] = gains[at : at + ro]
            grads[h, d] = g_stage[...].astype(bf16)


def layer(lengths, weights, tokens, cot, rd, ro):
    n_head, n_dp, rp = weights.shape[:3]
    tiles = tokens.shape[0] // B
    listed = tiles * (MAX_LEN // B + 1) + 2
    vmem = lambda shape, dtype: pltpu.VMEM(shape, dtype)
    scratch = [
        pltpu.SMEM((listed,), jnp.int32),
        pltpu.SMEM((listed,), jnp.int32),
        pltpu.SMEM((listed,), jnp.int32),
        vmem((HEADS, tiles, 1, B), f32),
        vmem((HEADS, 3 * HD, D), bf16),
        vmem((D, HEADS * 128), bf16),
        vmem((D, D), bf16),
        vmem((D, D), bf16),
        vmem((D, FF), bf16),
        vmem((FF, D), bf16),
        vmem((D, FF), bf16),
        vmem((FF, D), bf16),
        vmem((D, 128), f32),
        vmem((n_dp * rp, 128), f32),
        vmem((HEADS, tiles, 64, B), bf16),
        vmem((HEADS, tiles, HD, B), bf16),
        vmem((HEADS, tiles, 48, B), bf16),
        vmem((HEADS, tiles, B, 64), bf16),
        vmem((HEADS, tiles, B, 64), bf16),
        vmem((HEADS, tiles, 64, B), bf16),
        vmem((CAP + 2, HEADS, B, B), bf16),
        vmem((2, HEADS, B, B), bf16),
        vmem((HEADS, tiles, HD + 8, B), f32),
        vmem((HEADS, tiles, HD, B), f32),
        vmem((HEADS, tiles, HD, B), f32),
        vmem((tiles, D, B), f32),
        vmem((tiles, D, B), bf16),
        vmem((2, B, B), bf16),
        vmem((HEADS, 1, B), f32),
        vmem((HEADS, 1, B), f32),
        vmem((D, HEADS * 128), f32),
        vmem((D, D), f32),
        vmem((D, FF), f32),
        vmem((D, FF), f32),
        vmem((4, D, 128), f32),
        vmem((rp, 128), f32),
    ]
    whole = pl.BlockSpec(memory_space=pltpu.VMEM)
    return pl.pallas_call(
        functools.partial(layer_kernel, rd, ro),
        out_shape=(
            jax.ShapeDtypeStruct(tokens.shape, bf16),
            jax.ShapeDtypeStruct(tokens.shape, bf16),
            jax.ShapeDtypeStruct((n_head, n_dp, rp, 128), bf16),
        ),
        in_specs=[pl.BlockSpec(memory_space=pltpu.SMEM), whole, whole, whole],
        out_specs=(whole, whole, whole),
        scratch_shapes=scratch,
        compiler_params=pltpu.CompilerParams(vmem_limit_bytes=62 * 1024 * 1024),
    )(lengths, weights, tokens, cot)


def factors(n_dp, n_head):
    dp, left = [], n_dp
    while left > 1:
        size = 4 if left % 4 == 0 else left
        dp.append(size)
        left //= size
    head = [2, 2] if n_head == 4 and n_dp == 8 else [n_head]
    out = []
    for axis, sizes in (("head", head), ("dp", dp)):
        stride = math.prod(sizes)
        for size in sizes:
            stride //= size
            out.append((axis, stride, size))
    return out


def digit(axis, stride, size):
    return lax.rem(lax.div(lax.axis_index(axis), stride), size)


def peer(axis, stride, size, offset):
    mine = digit(axis, stride, size)
    theirs = lax.rem(mine + offset, size)
    return {axis: lax.axis_index(axis) + (theirs - mine) * stride}, theirs


def greet(peers):
    barrier = pltpu.get_barrier_semaphore()
    for device in peers:
        pl.semaphore_signal(barrier, inc=1, device_id=device, device_id_type=MESH)
    pl.semaphore_wait(barrier, len(peers))


def gather_kernel(axes, qkv, out, up, down, norm, w_ref, stage, send, recv):
    rd, ro = qkv.shape[0], out.shape[0]
    greet([peer(*axis, o)[0] for axis in axes for o in range(1, axis[2])])
    stage[...] = jnp.zeros_like(stage)
    stage[0:rd, : qkv.shape[1]] = qkv[...]
    stage[rd : 2 * rd, : up.shape[1]] = up[...]
    stage[2 * rd : 3 * rd, : down.shape[1]] = down[...]
    stage[3 * rd : 3 * rd + ro] = out[...]
    stage[3 * rd + ro : 3 * rd + 2 * ro, : norm.shape[1]] = norm[...]
    mine = [digit(*axis) for axis in axes]
    w_ref[tuple(mine)] = stage[...].astype(bf16)
    have = list(mine)
    n = 0
    for a in reversed(range(len(axes))):
        copies = []
        for o in range(1, axes[a][2]):
            device, _ = peer(*axes[a], o)
            block = w_ref.at[tuple(have)]
            _, source = peer(*axes[a], axes[a][2] - o)
            there = list(have)
            there[a] = source
            copies.append(
                (
                    pltpu.make_async_remote_copy(
                        src_ref=block,
                        dst_ref=block,
                        send_sem=send.at[n],
                        recv_sem=recv.at[n],
                        device_id=device,
                        device_id_type=MESH,
                    ),
                    pltpu.make_async_remote_copy(
                        src_ref=w_ref.at[tuple(there)],
                        dst_ref=w_ref.at[tuple(there)],
                        send_sem=send.at[n],
                        recv_sem=recv.at[n],
                        device_id=device,
                        device_id_type=MESH,
                    ),
                )
            )
            n += 1
        for out_copy, _ in copies:
            out_copy.start()
        for out_copy, in_copy in copies:
            in_copy.wait_recv()
            out_copy.wait_send()
        have[a] = slice(None)


def gather(axes, rows, masters):
    copies = sum(size - 1 for _, _, size in axes)
    whole = pl.BlockSpec(memory_space=pltpu.VMEM)
    shape = tuple(size for _, _, size in axes) + (rows, 128)
    return pl.pallas_call(
        functools.partial(gather_kernel, axes),
        out_shape=jax.ShapeDtypeStruct(shape, bf16),
        in_specs=[whole] * 5,
        out_specs=whole,
        scratch_shapes=[
            pltpu.VMEM((rows, 128), f32),
            pltpu.SemaphoreType.DMA((copies,)),
            pltpu.SemaphoreType.DMA((copies,)),
        ],
        compiler_params=pltpu.CompilerParams(
            collective_id=0, has_side_effects=True, vmem_limit_bytes=32 * 1024 * 1024
        ),
    )(*masters)


def scatter_kernel(axes, groups, g_ref, red_ref, sq_ref, *scratch):
    stages = len(axes)
    arrived = scratch[:stages]
    partial = scratch[stages : 2 * stages - 1]
    squares, (send, recv) = scratch[2 * stages - 1 : -2], scratch[-2:]
    greet([peer(*group, o)[0] for group in groups for o in range(1, group[2])])
    current = g_ref
    n = 0
    for s, a in enumerate(reversed(range(len(axes)))):
        order = current.shape[:-2]
        lead = (slice(None),) * (len(order) - 1)
        copies = []
        for o in range(1, axes[a][2]):
            device, theirs = peer(*axes[a], o)
            copies.append(
                pltpu.make_async_remote_copy(
                    src_ref=current.at[lead + (theirs,)],
                    dst_ref=arrived[s].at[o - 1],
                    send_sem=send.at[n],
                    recv_sem=recv.at[n],
                    device_id=device,
                    device_id_type=MESH,
                )
            )
            n += 1
        for copy in copies:
            copy.start()
        total = current[lead + (digit(*axes[a]),)].astype(f32)
        for o, copy in enumerate(copies):
            copy.wait_recv()
            total = total + arrived[s][o].astype(f32)
        for copy in copies:
            copy.wait_send()
        if s < stages - 1:
            partial[s][...] = total.astype(bf16)
            current = partial[s]
    red_ref[...] = total
    square = total * total
    fold = square[0:8]
    for r in range(8, square.shape[0], 8):
        fold = fold + square[r : r + 8]
    for group, ref in zip(groups, squares):
        mine = digit(*group)
        ref[mine] = fold
        copies = []
        for o in range(1, group[2]):
            device, _ = peer(*group, o)
            _, source = peer(*group, group[2] - o)
            make = lambda at, device=device, n=n: pltpu.make_async_remote_copy(
                src_ref=ref.at[at],
                dst_ref=ref.at[at],
                send_sem=send.at[n],
                recv_sem=recv.at[n],
                device_id=device,
                device_id_type=MESH,
            )
            copies.append((make(mine), make(source)))
            n += 1
        for out_copy, _ in copies:
            out_copy.start()
        for out_copy, in_copy in copies:
            in_copy.wait_recv()
            out_copy.wait_send()
        fold = ref[0]
        for j in range(1, group[2]):
            fold = fold + ref[j]
    sq_ref[...] = fold


def scatter(axes, groups, grads):
    sizes = [size for _, _, size in axes]
    block = grads.shape[-2:]
    arrived, partial = [], []
    for a in reversed(range(len(axes))):
        arrived.append(pltpu.VMEM((sizes[a] - 1,) + tuple(sizes[:a]) + block, bf16))
        if a:
            partial.append(pltpu.VMEM(tuple(sizes[:a]) + block, bf16))
    squares = [pltpu.VMEM((size, 8, 128), f32) for _, _, size in groups]
    copies = sum(size - 1 for size in sizes) + sum(size - 1 for _, _, size in groups)
    whole = pl.BlockSpec(memory_space=pltpu.VMEM)
    return pl.pallas_call(
        functools.partial(scatter_kernel, axes, groups),
        out_shape=(jax.ShapeDtypeStruct(block, f32), jax.ShapeDtypeStruct((8, 128), f32)),
        in_specs=[whole],
        out_specs=(whole, whole),
        scratch_shapes=arrived
        + partial
        + squares
        + [pltpu.SemaphoreType.DMA((copies,)), pltpu.SemaphoreType.DMA((copies,))],
        compiler_params=pltpu.CompilerParams(
            collective_id=1, has_side_effects=True, vmem_limit_bytes=32 * 1024 * 1024
        ),
    )(grads)


def adam(weight, first, second, grad, factor, rate, decay):
    clipped = grad * factor
    first_new = BETA_ONE * first + (1.0 - BETA_ONE) * clipped
    second_new = BETA_TWO * second + (1.0 - BETA_TWO) * clipped * clipped
    direction = (
        first_new
        / (1.0 - BETA_ONE**STEP)
        / (jnp.sqrt(second_new / (1.0 - BETA_TWO**STEP)) + ADAM_EPS)
    )
    return weight - rate * (direction + decay * weight), first_new, second_new


def update_kernel(red, sq, *refs):
    params, outs = refs[:15], refs[15:]
    rd, ro = params[0].shape[0], params[1].shape[0]
    norm = jnp.sqrt(jnp.sum(sq[...], keepdims=True))
    outs[0][...] = norm
    factor = jnp.minimum(1.0, CLIP_NORM / norm)
    rows = (0, 3 * rd, rd, 2 * rd, 3 * rd + ro)
    rates = (0.1, 0.5, 0.1, 0.1, 0.5)
    decays = (DECAY, DECAY, DECAY, DECAY, 0.0)
    for w in range(5):
        height, width = params[w].shape
        grad = red[rows[w] : rows[w] + height, :width]
        new, first_new, second_new = adam(
            params[w][...], params[5 + w][...], params[10 + w][...], grad, factor, rates[w], decays[w]
        )
        outs[1 + 3 * w][...] = new
        outs[2 + 3 * w][...] = first_new
        outs[3 + 3 * w][...] = second_new
        outs[16 + w][...] = grad
        outs[21 + w][...] = new.astype(bf16)


def update(red, sq, params):
    whole = pl.BlockSpec(memory_space=pltpu.VMEM)
    like = lambda p, dtype: jax.ShapeDtypeStruct(p.shape, dtype)
    shapes = [jax.ShapeDtypeStruct((1, 1), f32)]
    shapes += [like(p, f32) for p in params[:5] for _ in range(3)]
    shapes += [like(p, f32) for p in params[:5]]
    shapes += [like(p, bf16) for p in params[:5]]
    return pl.pallas_call(
        update_kernel,
        out_shape=shapes,
        in_specs=[whole] * 17,
        out_specs=[whole] * len(shapes),
        compiler_params=pltpu.CompilerParams(vmem_limit_bytes=32 * 1024 * 1024),
    )(red, sq, *params)


def per_device(n_dp, n_head, tokens, cotangent, lengths, *params):
    masters = params[:5]
    rd, ro = masters[0].shape[0], masters[1].shape[0]
    rows = -(-(3 * rd + 2 * ro) // 16) * 16
    axes = factors(n_dp, n_head)
    groups = [("dp", 1, n_dp), ("head", 1, n_head)]
    weights = gather(axes, rows, masters).reshape(n_head, n_dp, rows, 128)
    mixed, input_grad, grads = layer(lengths, weights, tokens, cotangent, rd, ro)
    grads = grads.reshape(tuple(size for _, _, size in axes) + (rows, 128))
    red, sq = scatter(axes, groups, grads)
    outs = update(red, sq, params)
    return (mixed, input_grad, outs[0].reshape(()), *outs[1:])


def solution(mesh):
    both, split, lens = P(("dp", "head"), None), P("dp", "head"), P("dp", None)
    weight = (split, both, split, split, both)
    return jax.shard_map(
        functools.partial(per_device, mesh.shape["dp"], mesh.shape["head"]),
        mesh=mesh,
        in_specs=(both, both, lens) + weight * 3,
        out_specs=(both, both, P())
        + tuple(spec for spec in weight for _ in range(3))
        + weight
        + weight,
        check_vma=False,
    )
```

time: 1490 us -> 150 us (0.10); the launches traced: 1470 us -> 152 us
  matrix products: 501 us -> 0 us
  blocking collectives: 261 us -> 0 us
  loops' own time: 251 us -> 0 us
  waiting for transfers between devices: 161 us -> 0 us
  local copies, waits for them, and re-layouts: 159 us -> 5.9 us
  Pallas kernels: 0 us -> 145 us
  other arithmetic: 104 us -> 0 us
  between operations: 20.5 us -> 0.91 us
    dot_general x236 -> x0, matrix products: 501 us -> none  [the longest x168 357 us: contract(): lax.dot_general(left, right, (((left_dim,), (right_dim,)), ((), ())), pre...]
    another operation x2 -> x0, loops' own time: 251 us -> none  [the longest x1 126 us: attend_forward(): result, log_total = lax.map(one, starts)]
    all_gather x5 -> x0, blocking collectives: 181 us -> none  [the longest x1 46 us: per_device(): lax.all_gather(out_master.astype(jnp.bfloat16), ('dp', 'head'), axis=0, t...]
    reduce_scatter x6 -> x0, waiting for transfers between devices: 152 us -> none  [the longest x1 44.9 us: per_device(): lax.psum_scatter(contract(part, w_down, 1, 1).astype(jnp.bfloat16), 'head...]
    pallas_call x0 -> x4, Pallas kernels: none -> 145 us  [the longest x1 88 us: layer(): pl.pallas_call(functools.partial(layer_kernel, rd, ro), out_shape=(jax.Sh...]
    dynamic_slice x224 -> x0, local copies, waits for them, and re-layouts: 49.8 us -> none  [the longest x64 37.4 us: attend_forward(): result, log_total = lax.map(one, starts)]
    add x161 -> x0, other arithmetic: 45.4 us -> none  [the longest x64 41.5 us: window(): query_place = start + jnp.arange(BLOCK, dtype=jnp.int32)]
    psum x1 -> x0, blocking collectives: 40.9 us -> none  [per_device(): total_square = lax.psum(local_square, ('dp', 'head'))]
  transfers between devices with their start and end apart: 12 -> 0, of which waited for: 5 -> 0; matrix products, arithmetic and copies ran while one was open for 33% -> 0% of each run, Pallas kernels for 0% -> 0%
where the time goes in v1:
time: 150 us; the launch traced here: 152 us
  Pallas kernels  145 us (97%)
  local copies, waits for them, and re-layouts  5.9 us (4%)
    pallas_call x1, Pallas kernels, layer(): pl.pallas_call(functools.partial(layer_kernel, rd, ro), out_shape=(jax.Sh...  88 us
    pallas_call x1, Pallas kernels, scatter(): pl.pallas_call(functools.partial(scatter_kernel, axes, groups), out_shape...  35.8 us
    pallas_call x1, Pallas kernels, gather(): pl.pallas_call(functools.partial(gather_kernel, axes), out_shape=jax.Shap...  20.8 us
    unnamed x44, local copies, waits for them, and re-layouts  5.9 us

profile of v1, /device:TPU:0, one launch (start us, length us, event | category | flops | bytes accessed | tf_op | source)
XLA Modules:
  0.0 152.3 jit_solution(13215853624505386205)
XLA Ops:
  0.7 0.0 copy-start.2
  0.7 0.7 copy-done.2
  1.4 0.7 copy-done.4
  2.1 0.7 copy-done.6
  2.8 0.7 copy-done.8
  3.4 0.7 copy-done.10
  4.1 20.8 %shard_map.393 = bf16[2,2,4,2,64,128]{5,4,3,2,1,0:T(8,128)(2,1)S(1)} custom-call(f32[16,96]{1,0:T(8,128)S(1)} %copy-done.2, f32[4,128]{1,0:T(4,128)S(1)} %copy-done.8, f32[16,128]{1,0:T(8,128)S(1)} %copy-done.4, f32[16,128]{1,0:T(8,128)S(1)} %copy-done.6, f32[4,4]{1,0:T(4,128)S(1)} %copy-done.10), custom_call_target="tpu_custom_call" | custom-call | tf_op jit(solution)/shard_map/pallas_call | solution.py:514
  25.0 0.0 copy-start
  25.0 0.8 copy-done
  25.8 88.0 %shard_map.394 = (bf16[4096,128]{1,0:T(8,128)(2,1)}, bf16[4096,128]{1,0:T(8,128)(2,1)}, bf16[4,8,64,128]{3,2,1,0:T(8,128)(2,1)}) custom-call(s32[4,8]{1,0:T(4,128)} %lengths.1, bf16[4,8,64,128]{3,2,1,0:T(8,128)(2,1)} %bitcast.3, bf16[4096,128]{1,0:T(8,128)(2,1)} %tokens.1, bf16[4096,128]{1,0:T(8,128)(2,1)} %cot.1), custom_call_target="tpu_custom_call" | custom-call | tf_op jit(solution)/shard_map/pallas_call | solution.py:413
  113.8 1.0 copy-done.1
  114.8 0.0 copy-start.12
  114.8 0.0 copy-start.13
  114.8 0.0 copy-start.14
  114.8 0.0 copy-start.15
  114.9 0.0 copy-start.16
  114.9 0.0 copy-start.17
  114.9 0.0 copy-start.18
  114.9 0.0 copy-start.19
  114.9 0.0 copy-start.20
  114.9 0.0 copy-start.21
  114.9 35.8 %shard_map.395 = (f32[64,128]{1,0:T(8,128)S(1)}, f32[8,128]{1,0:T(8,128)S(1)}) custom-call(bf16[2,2,4,2,64,128]{5,4,3,2,1,0:T(8,128)(2,1)S(1)} %bitcast.4), custom_call_target="tpu_custom_call" | custom-call | tf_op jit(solution)/shard_map/pallas_call | solution.py:610
  150.7 0.0 copy-start.9
  150.8 0.0 copy-done.3
  150.8 0.0 copy-done.5
  150.8 0.0 copy-done.7
  150.8 0.0 copy-done.11
  150.8 0.0 copy-done.12
  150.8 0.0 copy-done.13
  150.8 0.0 copy-done.14
  150.9 0.5 copy-done.9
  151.4 0.8 shard_map.396
  (16 shorter events, 0.0 us)
Async XLA Ops:
  0.7 0.7 copy-start.2
  1.4 0.7 copy-start.4
  2.1 0.7 copy-start.6
  2.8 0.7 copy-start.8
  3.4 0.7 copy-start.10
  25.0 0.8 copy-start
  113.7 1.0 copy-start.1
  114.8 36.0 %copy-start.3 = (f32[16,96]{1,0:T(8,128)S(1)}, f32[16,96]{1,0:T(8,128)}, u32[]{:S(2)}) copy-start(f32[16,96]{1,0:T(8,128)} %refs_0_.1) | copy-start | bytes 18436
  114.8 36.0 %copy-start.5 = (f32[16,128]{1,0:T(8,128)S(1)}, f32[16,128]{1,0:T(8,128)}, u32[]{:S(2)}) copy-start(f32[16,128]{1,0:T(8,128)} %refs_2_.1) | copy-start | bytes 24580
  114.8 36.0 %copy-start.7 = (f32[16,128]{1,0:T(8,128)S(1)}, f32[16,128]{1,0:T(8,128)}, u32[]{:S(2)}) copy-start(f32[16,128]{1,0:T(8,128)} %refs_3_.1) | copy-start | bytes 24580
  114.8 36.0 %copy-start.11 = (f32[4,4]{1,0:T(4,128)S(1)}, f32[4,4]{1,0:T(4,128)}, u32[]{:S(2)}) copy-start(f32[4,4]{1,0:T(4,128)} %refs_4_.1) | copy-start | bytes 196
  114.8 36.0 %copy-start.12 = (f32[16,96]{1,0:T(8,128)S(1)}, f32[16,96]{1,0:T(8,128)}, u32[]{:S(2)}) copy-start(f32[16,96]{1,0:T(8,128)} %refs_5_.1) | copy-start | bytes 18436
  114.8 36.0 %copy-start.13 = (f32[16,128]{1,0:T(8,128)S(1)}, f32[16,128]{1,0:T(8,128)}, u32[]{:S(2)}) copy-start(f32[16,128]{1,0:T(8,128)} %refs_7_.1) | copy-start | bytes 24580
  114.8 36.0 %copy-start.14 = (f32[16,128]{1,0:T(8,128)S(1)}, f32[16,128]{1,0:T(8,128)}, u32[]{:S(2)}) copy-start(f32[16,128]{1,0:T(8,128)} %refs_8_.1) | copy-start | bytes 24580
  114.8 36.0 %copy-start.15 = (f32[16,96]{1,0:T(8,128)S(1)}, f32[16,96]{1,0:T(8,128)}, u32[]{:S(2)}) copy-start(f32[16,96]{1,0:T(8,128)} %refs_10_.1) | copy-start | bytes 18436
  114.9 36.0 %copy-start.16 = (f32[16,128]{1,0:T(8,128)S(1)}, f32[16,128]{1,0:T(8,128)}, u32[]{:S(2)}) copy-start(f32[16,128]{1,0:T(8,128)} %refs_12_.1) | copy-start | bytes 24580
  114.9 36.0 %copy-start.17 = (f32[16,128]{1,0:T(8,128)S(1)}, f32[16,128]{1,0:T(8,128)}, u32[]{:S(2)}) copy-start(f32[16,128]{1,0:T(8,128)} %refs_13_.1) | copy-start | bytes 24580
  114.9 36.0 %copy-start.18 = (f32[4,128]{1,0:T(4,128)S(1)}, f32[4,128]{1,0:T(4,128)}, u32[]{:S(2)}) copy-start(f32[4,128]{1,0:T(4,128)} %refs_6_.1) | copy-start | bytes 6148
  114.9 36.0 %copy-start.19 = (f32[4,4]{1,0:T(4,128)S(1)}, f32[4,4]{1,0:T(4,128)}, u32[]{:S(2)}) copy-start(f32[4,4]{1,0:T(4,128)} %refs_9_.1) | copy-start | bytes 196
  114.9 36.0 %copy-start.20 = (f32[4,128]{1,0:T(4,128)S(1)}, f32[4,128]{1,0:T(4,128)}, u32[]{:S(2)}) copy-start(f32[4,128]{1,0:T(4,128)} %refs_11_.1) | copy-start | bytes 6148
  114.9 36.0 %copy-start.21 = (f32[4,4]{1,0:T(4,128)S(1)}, f32[4,4]{1,0:T(4,128)}, u32[]{:S(2)}) copy-start(f32[4,4]{1,0:T(4,128)} %refs_14_.1) | copy-start | bytes 196
  150.7 0.7 copy-start.9

commit v2 on v1

--- a/solution.py
+++ b/solution.py
@@ -1,4 +1,5 @@
 import functools
+import itertools
 import math
 
 import jax
@@ -311,6 +312,7 @@
     acc[...] = jnp.zeros_like(acc)
 
     def backward(t, carry):
+        pl.when(us[t] > CAP)(lambda: weigh(t, us[t]))
         i, j = uq[t - 1], uk[t - 1]
         old = lax.rem(t - 1, 2)
         for h in range(HEADS):
@@ -318,7 +320,6 @@
             acc[h, i, :HD] += mm(kf[h, j], sg)
             dk_acc[h, j] += mm_nt(qf[h, i, :HD], sg)
         i, j, slot = uq[t], uk[t], us[t]
-        pl.when(slot > CAP)(lambda: weigh(t, slot))
         new = lax.rem(t, 2)
         for h in range(HEADS):
             p = probs[slot, h]
@@ -425,142 +426,168 @@
 
 
 def factors(n_dp, n_head):
-    dp, left = [], n_dp
+    if (n_dp, n_head) == (8, 4):
+        axes = (("head", 2, 2), ("head", 1, 2), ("dp", 2, 4), ("dp", 1, 2))
+        return axes, ((2,), (0, 3), (1,)), ((1,), (0, 3), (2,)), ((1,), (0, 2, 3))
+    axes, left = [("head", 1, n_head)], n_dp
     while left > 1:
         size = 4 if left % 4 == 0 else left
-        dp.append(size)
         left //= size
-    head = [2, 2] if n_head == 4 and n_dp == 8 else [n_head]
-    out = []
-    for axis, sizes in (("head", head), ("dp", dp)):
-        stride = math.prod(sizes)
-        for size in sizes:
-            stride //= size
-            out.append((axis, stride, size))
-    return out
+        axes.append(("dp", left, size))
+    each = tuple((a,) for a in range(len(axes)))
+    return tuple(axes), each[::-1], each, each
 
 
 def digit(axis, stride, size):
     return lax.rem(lax.div(lax.axis_index(axis), stride), size)
 
 
-def peer(axis, stride, size, offset):
-    mine = digit(axis, stride, size)
-    theirs = lax.rem(mine + offset, size)
-    return {axis: lax.axis_index(axis) + (theirs - mine) * stride}, theirs
+def others(axes, group):
+    found = []
+    for offsets in itertools.product(*(range(axes[a][2]) for a in group)):
+        if not any(offsets):
+            continue
+        place, theirs, source = {}, {}, {}
+        for a, offset in zip(group, offsets):
+            axis, stride, size = axes[a]
+            mine = digit(*axes[a])
+            theirs[a] = lax.rem(mine + offset, size)
+            source[a] = lax.rem(mine + size - offset, size)
+            place[axis] = place.get(axis, lax.axis_index(axis)) + (theirs[a] - mine) * stride
+        found.append((place, theirs, source))
+    return found
 
 
 def greet(peers):
     barrier = pltpu.get_barrier_semaphore()
     for device in peers:
         pl.semaphore_signal(barrier, inc=1, device_id=device, device_id_type=MESH)
-    pl.semaphore_wait(barrier, len(peers))
-
-
-def gather_kernel(axes, qkv, out, up, down, norm, w_ref, stage, send, recv):
+    return lambda: pl.semaphore_wait(barrier, len(peers))
+
+
+def remote(src, dst, sems, n, device):
+    return pltpu.make_async_remote_copy(
+        src_ref=src,
+        dst_ref=dst,
+        send_sem=sems[0].at[n],
+        recv_sem=sems[1].at[n],
+        device_id=device,
+        device_id_type=MESH,
+    )
+
+
+def peers_of(axes, groups):
+    return [place for group in groups for place, _, _ in others(axes, group)]
+
+
+def gather_kernel(axes, groups, *refs):
+    masters, w_ref = refs[:5], refs[5]
+    held, (stage, block, local, send, recv) = refs[6:11], refs[11:]
+    arrived = greet(peers_of(axes, groups))
+    loads = [pltpu.make_async_copy(m, h, local.at[n]) for n, (m, h) in enumerate(zip(masters, held))]
+    for load in loads:
+        load.start()
+    stage[...] = jnp.zeros_like(stage)
+    for load in loads:
+        load.wait()
+    qkv, out, up, down, norm = held
     rd, ro = qkv.shape[0], out.shape[0]
-    greet([peer(*axis, o)[0] for axis in axes for o in range(1, axis[2])])
-    stage[...] = jnp.zeros_like(stage)
-    stage[0:rd, : qkv.shape[1]] = qkv[...]
-    stage[rd : 2 * rd, : up.shape[1]] = up[...]
-    stage[2 * rd : 3 * rd, : down.shape[1]] = down[...]
-    stage[3 * rd : 3 * rd + ro] = out[...]
-    stage[3 * rd + ro : 3 * rd + 2 * ro, : norm.shape[1]] = norm[...]
-    mine = [digit(*axis) for axis in axes]
-    w_ref[tuple(mine)] = stage[...].astype(bf16)
-    have = list(mine)
-    n = 0
-    for a in reversed(range(len(axes))):
-        copies = []
-        for o in range(1, axes[a][2]):
-            device, _ = peer(*axes[a], o)
-            block = w_ref.at[tuple(have)]
-            _, source = peer(*axes[a], axes[a][2] - o)
+    at = 0
+    for part, height in ((qkv, rd), (up, rd), (down, rd), (out, ro), (norm, ro)):
+        stage[at : at + height, : part.shape[1]] = part[...]
+        at += height
+    block[...] = stage[...].astype(bf16)
+    have = [digit(*axis) for axis in axes]
+    keep = pltpu.make_async_copy(block, w_ref.at[tuple(have)], local.at[0])
+    keep.start()
+    arrived()
+    sent, n = [], 0
+    for group in groups:
+        coming = []
+        for place, _, source in others(axes, group):
+            mine = w_ref.at[tuple(have)]
+            copy = remote(block if n < len(others(axes, groups[0])) else mine, mine, (send, recv), n, place)
+            copy.start()
+            sent.append(copy)
             there = list(have)
-            there[a] = source
-            copies.append(
-                (
-                    pltpu.make_async_remote_copy(
-                        src_ref=block,
-                        dst_ref=block,
-                        send_sem=send.at[n],
-                        recv_sem=recv.at[n],
-                        device_id=device,
-                        device_id_type=MESH,
-                    ),
-                    pltpu.make_async_remote_copy(
-                        src_ref=w_ref.at[tuple(there)],
-                        dst_ref=w_ref.at[tuple(there)],
-                        send_sem=send.at[n],
-                        recv_sem=recv.at[n],
-                        device_id=device,
-                        device_id_type=MESH,
-                    ),
-                )
-            )
+            for a in group:
+                there[a] = source[a]
+            there = w_ref.at[tuple(there)]
+            coming.append(remote(there, there, (send, recv), n, place))
             n += 1
-        for out_copy, _ in copies:
-            out_copy.start()
-        for out_copy, in_copy in copies:
-            in_copy.wait_recv()
-            out_copy.wait_send()
-        have[a] = slice(None)
-
-
-def gather(axes, rows, masters):
-    copies = sum(size - 1 for _, _, size in axes)
-    whole = pl.BlockSpec(memory_space=pltpu.VMEM)
+        if group is groups[0]:
+            keep.wait()
+        for copy in coming:
+            copy.wait_recv()
+        for a in group:
+            have[a] = slice(None)
+    for copy in sent:
+        copy.wait_send()
+
+
+ANY = pl.BlockSpec(memory_space=pl.ANY)
+WHOLE = pl.BlockSpec(memory_space=pltpu.VMEM)
+
+
+def copies_of(axes, groups):
+    return sum(math.prod(axes[a][2] for a in group) - 1 for group in groups)
+
+
+def gather(axes, groups, rows, masters, cid=0, out=ANY):
+    copies = copies_of(axes, groups)
     shape = tuple(size for _, _, size in axes) + (rows, 128)
     return pl.pallas_call(
-        functools.partial(gather_kernel, axes),
+        functools.partial(gather_kernel, axes, groups),
         out_shape=jax.ShapeDtypeStruct(shape, bf16),
-        in_specs=[whole] * 5,
-        out_specs=whole,
-        scratch_shapes=[
+        in_specs=[ANY] * 5,
+        out_specs=out,
+        scratch_shapes=[pltpu.VMEM(m.shape, f32) for m in masters]
+        + [
             pltpu.VMEM((rows, 128), f32),
+            pltpu.VMEM((rows, 128), bf16),
+            pltpu.SemaphoreType.DMA((5,)),
             pltpu.SemaphoreType.DMA((copies,)),
             pltpu.SemaphoreType.DMA((copies,)),
         ],
         compiler_params=pltpu.CompilerParams(
-            collective_id=0, has_side_effects=True, vmem_limit_bytes=32 * 1024 * 1024
+            collective_id=cid, has_side_effects=True, vmem_limit_bytes=32 * 1024 * 1024
         ),
     )(*masters)
 
 
-def scatter_kernel(axes, groups, g_ref, red_ref, sq_ref, *scratch):
-    stages = len(axes)
-    arrived = scratch[:stages]
-    partial = scratch[stages : 2 * stages - 1]
-    squares, (send, recv) = scratch[2 * stages - 1 : -2], scratch[-2:]
-    greet([peer(*group, o)[0] for group in groups for o in range(1, group[2])])
+def scatter_kernel(axes, groups, sums, g_ref, red_ref, sq_ref, *scratch):
+    own, scratch = scratch[0], scratch[1:]
+    arrived, scratch = scratch[: len(groups)], scratch[len(groups) :]
+    partial, scratch = scratch[: len(groups) - 1], scratch[len(groups) - 1 :]
+    squares, (local, send, recv) = scratch[:-3], scratch[-3:]
+    peers = peers_of(axes, groups) + [p for s in sums if s not in groups for p in peers_of(axes, [s])]
+    ready = greet(peers)
+    left = list(range(len(axes)))
+    pick = lambda digits: tuple(digits.get(a, slice(None)) for a in left)
+    mine = lambda group: {a: digit(*axes[a]) for a in group}
+    load = pltpu.make_async_copy(g_ref.at[pick(mine(groups[0]))], own, local.at[0])
+    load.start()
+    ready()
+    sent, n = [], 0
     current = g_ref
-    n = 0
-    for s, a in enumerate(reversed(range(len(axes)))):
-        order = current.shape[:-2]
-        lead = (slice(None),) * (len(order) - 1)
-        copies = []
-        for o in range(1, axes[a][2]):
-            device, theirs = peer(*axes[a], o)
-            copies.append(
-                pltpu.make_async_remote_copy(
-                    src_ref=current.at[lead + (theirs,)],
-                    dst_ref=arrived[s].at[o - 1],
-                    send_sem=send.at[n],
-                    recv_sem=recv.at[n],
-                    device_id=device,
-                    device_id_type=MESH,
-                )
-            )
+    for s, group in enumerate(groups):
+        coming = []
+        for o, (place, theirs, _) in enumerate(others(axes, group)):
+            copy = remote(current.at[pick(theirs)], arrived[s].at[o], (send, recv), n, place)
+            copy.start()
+            sent.append(copy)
+            coming.append(copy)
             n += 1
-        for copy in copies:
-            copy.start()
-        total = current[lead + (digit(*axes[a]),)].astype(f32)
-        for o, copy in enumerate(copies):
+        if s == 0:
+            load.wait()
+            total = own[...].astype(f32)
+        else:
+            total = current[pick(mine(group))].astype(f32)
+        for o, copy in enumerate(coming):
             copy.wait_recv()
             total = total + arrived[s][o].astype(f32)
-        for copy in copies:
-            copy.wait_send()
-        if s < stages - 1:
+        left = [a for a in left if a not in group]
+        if left:
             partial[s][...] = total.astype(bf16)
             current = partial[s]
     red_ref[...] = total
@@ -568,56 +595,56 @@
     fold = square[0:8]
     for r in range(8, square.shape[0], 8):
         fold = fold + square[r : r + 8]
-    for group, ref in zip(groups, squares):
-        mine = digit(*group)
-        ref[mine] = fold
-        copies = []
-        for o in range(1, group[2]):
-            device, _ = peer(*group, o)
-            _, source = peer(*group, group[2] - o)
-            make = lambda at, device=device, n=n: pltpu.make_async_remote_copy(
-                src_ref=ref.at[at],
-                dst_ref=ref.at[at],
-                send_sem=send.at[n],
-                recv_sem=recv.at[n],
-                device_id=device,
-                device_id_type=MESH,
-            )
-            copies.append((make(mine), make(source)))
+    fold = jnp.sum(fold, axis=0, keepdims=True)
+    for group, ref in zip(sums, squares):
+        digits = mine(group)
+        ref[tuple(digits[a] for a in group)] = fold
+        at = lambda digits: ref.at[tuple(digits[a] for a in group)]
+        coming = []
+        for place, _, source in others(axes, group):
+            copy = remote(at(digits), at(digits), (send, recv), n, place)
+            copy.start()
+            sent.append(copy)
+            coming.append(remote(at(source), at(source), (send, recv), n, place))
             n += 1
-        for out_copy, _ in copies:
-            out_copy.start()
-        for out_copy, in_copy in copies:
-            in_copy.wait_recv()
-            out_copy.wait_send()
-        fold = ref[0]
-        for j in range(1, group[2]):
-            fold = fold + ref[j]
+        for copy in coming:
+            copy.wait_recv()
+        fold = 0.0
+        for index in itertools.product(*(range(axes[a][2]) for a in group)):
+            fold = fold + ref[index]
     sq_ref[...] = fold
-
-
-def scatter(axes, groups, grads):
-    sizes = [size for _, _, size in axes]
+    for copy in sent:
+        copy.wait_send()
+
+
+def scatter(axes, groups, sums, grads, cid=1):
+    size = lambda a: axes[a][2]
     block = grads.shape[-2:]
+    left = list(range(len(axes)))
     arrived, partial = [], []
-    for a in reversed(range(len(axes))):
-        arrived.append(pltpu.VMEM((sizes[a] - 1,) + tuple(sizes[:a]) + block, bf16))
-        if a:
-            partial.append(pltpu.VMEM(tuple(sizes[:a]) + block, bf16))
-    squares = [pltpu.VMEM((size, 8, 128), f32) for _, _, size in groups]
-    copies = sum(size - 1 for size in sizes) + sum(size - 1 for _, _, size in groups)
-    whole = pl.BlockSpec(memory_space=pltpu.VMEM)
+    for group in groups:
+        left = [a for a in left if a not in group]
+        shape = tuple(size(a) for a in left) + block
+        arrived.append(pltpu.VMEM((math.prod(size(a) for a in group) - 1,) + shape, bf16))
+        partial.append(pltpu.VMEM(shape, bf16))
+    squares = [pltpu.VMEM(tuple(size(a) for a in group) + (1, 128), f32) for group in sums]
+    copies = copies_of(axes, groups) + copies_of(axes, sums)
     return pl.pallas_call(
-        functools.partial(scatter_kernel, axes, groups),
-        out_shape=(jax.ShapeDtypeStruct(block, f32), jax.ShapeDtypeStruct((8, 128), f32)),
-        in_specs=[whole],
-        out_specs=(whole, whole),
-        scratch_shapes=arrived
-        + partial
+        functools.partial(scatter_kernel, axes, groups, sums),
+        out_shape=(jax.ShapeDtypeStruct(block, f32), jax.ShapeDtypeStruct((1, 128), f32)),
+        in_specs=[ANY],
+        out_specs=(WHOLE, WHOLE),
+        scratch_shapes=[partial[0]]
+        + arrived
+        + partial[:-1]
         + squares
-        + [pltpu.SemaphoreType.DMA((copies,)), pltpu.SemaphoreType.DMA((copies,))],
+        + [
+            pltpu.SemaphoreType.DMA((1,)),
+            pltpu.SemaphoreType.DMA((copies,)),
+            pltpu.SemaphoreType.DMA((copies,)),
+        ],
         compiler_params=pltpu.CompilerParams(
-            collective_id=1, has_side_effects=True, vmem_limit_bytes=32 * 1024 * 1024
+            collective_id=cid, has_side_effects=True, vmem_limit_bytes=32 * 1024 * 1024
         ),
     )(grads)
 
@@ -676,12 +703,11 @@
     masters = params[:5]
     rd, ro = masters[0].shape[0], masters[1].shape[0]
     rows = -(-(3 * rd + 2 * ro) // 16) * 16
-    axes = factors(n_dp, n_head)
-    groups = [("dp", 1, n_dp), ("head", 1, n_head)]
-    weights = gather(axes, rows, masters).reshape(n_head, n_dp, rows, 128)
+    axes, inward, outward, sums = factors(n_dp, n_head)
+    weights = gather(axes, inward, rows, masters).reshape(n_head, n_dp, rows, 128)
     mixed, input_grad, grads = layer(lengths, weights, tokens, cotangent, rd, ro)
     grads = grads.reshape(tuple(size for _, _, size in axes) + (rows, 128))
-    red, sq = scatter(axes, groups, grads)
+    red, sq = scatter(axes, outward, sums, grads)
     outs = update(red, sq, params)
     return (mixed, input_grad, outs[0].reshape(()), *outs[1:])
 

time: 150 us -> 122 us (0.81); the launches traced: 152 us -> 122 us
  Pallas kernels: 145 us -> 115 us
    pallas_call x2, Pallas kernels: 56.7 us -> 32.5 us  [the longest x1 18.1 us: scatter(): pl.pallas_call(functools.partial(scatter_kernel, axes, groups, sums), out...]
    pallas_call x1, Pallas kernels: 88 us -> 81.5 us  [layer(): pl.pallas_call(functools.partial(layer_kernel, rd, ro), out_shape=(jax.Sh...]
where the time goes in v2:
time: 122 us
  Pallas kernels  115 us (94%)
  local copies, waits for them, and re-layouts  5.9 us (5%)
    pallas_call x1, Pallas kernels, layer(): pl.pallas_call(functools.partial(layer_kernel, rd, ro), out_shape=(jax.Sh...  81.5 us
    pallas_call x1, Pallas kernels, scatter(): pl.pallas_call(functools.partial(scatter_kernel, axes, groups, sums), out...  18.1 us
    pallas_call x1, Pallas kernels, gather(): pl.pallas_call(functools.partial(gather_kernel, axes, groups), out_shape=...  14.4 us
    unnamed x44, local copies, waits for them, and re-layouts  5.9 us

profile of v2, /device:TPU:0, one launch (start us, length us, event | category | flops | bytes accessed | tf_op | source)
XLA Modules:
  0.0 121.6 jit_solution(12252768792252913420)
XLA Ops:
  0.7 0.0 copy-start.2
  0.7 0.7 copy-done.2
  1.4 0.7 copy-done.4
  2.1 0.7 copy-done.6
  2.8 0.7 copy-done.8
  3.4 0.7 copy-done.10
  4.1 14.4 %shard_map.393 = bf16[2,2,4,2,64,128]{5,4,3,2,1,0:T(8,128)(2,1)S(1)} custom-call(f32[16,96]{1,0:T(8,128)S(1)} %copy-done.2, f32[4,128]{1,0:T(4,128)S(1)} %copy-done.8, f32[16,128]{1,0:T(8,128)S(1)} %copy-done.4, f32[16,128]{1,0:T(8,128)S(1)} %copy-done.6, f32[4,4]{1,0:T(4,128)S(1)} %copy-done.10), custom_call_target="tpu_custom_call" | custom-call | tf_op jit(solution)/shard_map/pallas_call | solution.py:539
  18.5 0.0 copy-start
  18.5 0.8 copy-done
  19.3 81.5 %shard_map.394 = (bf16[4096,128]{1,0:T(8,128)(2,1)}, bf16[4096,128]{1,0:T(8,128)(2,1)}, bf16[4,8,64,128]{3,2,1,0:T(8,128)(2,1)}) custom-call(s32[4,8]{1,0:T(4,128)} %lengths.1, bf16[4,8,64,128]{3,2,1,0:T(8,128)(2,1)} %bitcast.3, bf16[4096,128]{1,0:T(8,128)(2,1)} %tokens.1, bf16[4096,128]{1,0:T(8,128)(2,1)} %cot.1), custom_call_target="tpu_custom_call" | custom-call | tf_op jit(solution)/shard_map/pallas_call | solution.py:414
  100.8 1.0 copy-done.1
  101.9 0.0 copy-start.12
  101.9 0.0 copy-start.13
  101.9 0.0 copy-start.14
  101.9 0.0 copy-start.15
  101.9 0.0 copy-start.16
  101.9 0.0 copy-start.17
  101.9 0.0 copy-start.18
  101.9 0.0 copy-start.19
  102.0 0.0 copy-start.20
  102.0 0.0 copy-start.21
  102.0 18.1 %shard_map.395 = (f32[64,128]{1,0:T(8,128)S(1)}, f32[1,128]{1,0:T(1,128)S(1)}) custom-call(bf16[2,2,4,2,64,128]{5,4,3,2,1,0:T(8,128)(2,1)S(1)} %bitcast.4), custom_call_target="tpu_custom_call" | custom-call | tf_op jit(solution)/shard_map/pallas_call | solution.py:632
  120.1 0.0 copy-start.9
  120.1 0.0 copy-done.3
  120.1 0.0 copy-done.5
  120.1 0.0 copy-done.7
  120.1 0.0 copy-done.11
  120.1 0.0 copy-done.12
  120.1 0.0 copy-done.13
  120.2 0.0 copy-done.14
  120.2 0.5 copy-done.9
  120.8 0.8 shard_map.396
  (16 shorter events, 0.0 us)
Async XLA Ops:
  0.7 0.7 copy-start.2
  1.4 0.7 copy-start.4
  2.1 0.7 copy-start.6
  2.8 0.7 copy-start.8
  3.4 0.7 copy-start.10
  18.5 0.8 copy-start
  100.8 1.0 copy-start.1
  101.8 18.2 %copy-start.3 = (f32[16,96]{1,0:T(8,128)S(1)}, f32[16,96]{1,0:T(8,128)}, u32[]{:S(2)}) copy-start(f32[16,96]{1,0:T(8,128)} %refs_0_.3) | copy-start | bytes 18436
  101.9 18.3 %copy-start.5 = (f32[16,128]{1,0:T(8,128)S(1)}, f32[16,128]{1,0:T(8,128)}, u32[]{:S(2)}) copy-start(f32[16,128]{1,0:T(8,128)} %refs_2_.3) | copy-start | bytes 24580
  101.9 18.3 %copy-start.7 = (f32[16,128]{1,0:T(8,128)S(1)}, f32[16,128]{1,0:T(8,128)}, u32[]{:S(2)}) copy-start(f32[16,128]{1,0:T(8,128)} %refs_3_.3) | copy-start | bytes 24580
  101.9 18.3 %copy-start.11 = (f32[4,4]{1,0:T(4,128)S(1)}, f32[4,4]{1,0:T(4,128)}, u32[]{:S(2)}) copy-start(f32[4,4]{1,0:T(4,128)} %refs_4_.3) | copy-start | bytes 196
  101.9 18.3 %copy-start.12 = (f32[16,96]{1,0:T(8,128)S(1)}, f32[16,96]{1,0:T(8,128)}, u32[]{:S(2)}) copy-start(f32[16,96]{1,0:T(8,128)} %refs_5_.1) | copy-start | bytes 18436
  101.9 18.3 %copy-start.13 = (f32[16,128]{1,0:T(8,128)S(1)}, f32[16,128]{1,0:T(8,128)}, u32[]{:S(2)}) copy-start(f32[16,128]{1,0:T(8,128)} %refs_7_.1) | copy-start | bytes 24580
  101.9 18.3 %copy-start.14 = (f32[16,128]{1,0:T(8,128)S(1)}, f32[16,128]{1,0:T(8,128)}, u32[]{:S(2)}) copy-start(f32[16,128]{1,0:T(8,128)} %refs_8_.1) | copy-start | bytes 24580
  101.9 18.3 %copy-start.15 = (f32[16,96]{1,0:T(8,128)S(1)}, f32[16,96]{1,0:T(8,128)}, u32[]{:S(2)}) copy-start(f32[16,96]{1,0:T(8,128)} %refs_10_.1) | copy-start | bytes 18436
  101.9 18.3 %copy-start.16 = (f32[16,128]{1,0:T(8,128)S(1)}, f32[16,128]{1,0:T(8,128)}, u32[]{:S(2)}) copy-start(f32[16,128]{1,0:T(8,128)} %refs_12_.1) | copy-start | bytes 24580
  101.9 18.3 %copy-start.17 = (f32[16,128]{1,0:T(8,128)S(1)}, f32[16,128]{1,0:T(8,128)}, u32[]{:S(2)}) copy-start(f32[16,128]{1,0:T(8,128)} %refs_13_.1) | copy-start | bytes 24580
  101.9 18.3 %copy-start.18 = (f32[4,128]{1,0:T(4,128)S(1)}, f32[4,128]{1,0:T(4,128)}, u32[]{:S(2)}) copy-start(f32[4,128]{1,0:T(4,128)} %refs_6_.1) | copy-start | bytes 6148
  101.9 18.3 %copy-start.19 = (f32[4,4]{1,0:T(4,128)S(1)}, f32[4,4]{1,0:T(4,128)}, u32[]{:S(2)}) copy-start(f32[4,4]{1,0:T(4,128)} %refs_9_.1) | copy-start | bytes 196
  102.0 18.3 %copy-start.20 = (f32[4,128]{1,0:T(4,128)S(1)}, f32[4,128]{1,0:T(4,128)}, u32[]{:S(2)}) copy-start(f32[4,128]{1,0:T(4,128)} %refs_11_.1) | copy-start | bytes 6148
  102.0 18.3 %copy-start.21 = (f32[4,4]{1,0:T(4,128)S(1)}, f32[4,4]{1,0:T(4,128)}, u32[]{:S(2)}) copy-start(f32[4,4]{1,0:T(4,128)} %refs_14_.1) | copy-start | bytes 196
  120.1 0.7 copy-start.9

commit v3 on v2

--- a/solution.py
+++ b/solution.py
@@ -23,14 +23,16 @@
 FF = 512
 B = 256
 CAP = 50
+WIDE = 2 * B
 BIG = 2.0**100
 LIMIT = 88.0
 MASKED = -1e30
-LN2 = math.log(2.0)
-QSCALE = HD**-0.5 / LN2
+SCALE = HD**-0.5 / math.log(2.0)
 f32 = jnp.float32
 bf16 = jnp.bfloat16
 MESH = pl.DeviceIdType.MESH
+ANY = pl.BlockSpec(memory_space=pl.ANY)
+WHOLE = pl.BlockSpec(memory_space=pltpu.VMEM)
 
 
 def mm(a, b):
@@ -69,19 +71,36 @@
     return out
 
 
+def together(steps, tiles):
+    def pair(p, carry):
+        running = [steps(p, half) for half in range(2)]
+        while running:
+            running = [r for r in running if next(r, "done") != "done"]
+        return carry
+
+    lax.fori_loop(0, tiles // 2, pair, 0)
+
+
 def layer_kernel(
     rd,
     ro,
     lengths,
+    w_hbm,
+    tokens_hbm,
+    cot_hbm,
+    mixed_hbm,
+    igrad_hbm,
+    grads_hbm,
+    uq,
+    uk,
+    us,
     w_ref,
     tokens,
     cot,
-    mixed,
-    igrad,
+    result,
     grads,
-    uq,
-    uk,
-    us,
+    loads,
+    stores,
     bounds,
     wqkv_t,
     wqkv,
@@ -106,6 +125,12 @@
     dv_acc,
     resid_grad,
     first,
+    cot_s,
+    heads_s,
+    second_s,
+    low_s,
+    hidden_s,
+    pre_s,
     causal,
     qn,
     kn,
@@ -116,20 +141,74 @@
     g_norm,
     g_stage,
 ):
-    n_head, n_dp = w_ref.shape[:2]
+    n_head, n_dp, rp = w_ref.shape[:3]
     tiles = tokens.shape[0] // B
     row = lax.rem(lax.axis_index("head"), n_head)
-
+    load = [
+        pltpu.make_async_copy(src, dst, loads.at[n])
+        for n, (src, dst) in enumerate(((w_hbm, w_ref), (tokens_hbm, tokens), (cot_hbm, cot)))
+    ]
+    for copy in load:
+        copy.start()
+
+    starts, ends = [], []
+    at = jnp.int32(0)
+    for s in range(lengths.shape[1]):
+        starts.append(at)
+        at = at + lengths[row, s]
+        ends.append(at)
+    place = lax.broadcasted_iota(jnp.int32, (8, B), 0)
+    start_v = jnp.zeros((8, B), jnp.int32)
+    end_v = jnp.zeros((8, B), jnp.int32)
+    for s in range(8):
+        start_v = jnp.where(place == s, starts[s], start_v)
+        end_v = jnp.where(place == s, ends[s], end_v)
+
+    def kept(t):
+        return jnp.where(t - 1 <= CAP, t - 1, CAP + 1 + lax.rem(t, 2))
+
+    def blank(t, carry):
+        uq[t] = 0
+        uk[t] = 0
+        us[t] = 0
+        return carry
+
+    def list_q(i, n):
+        low = jnp.int32(0)
+        for s in range(1, 8):
+            low = jnp.where(starts[s] <= i * B, starts[s], low)
+
+        def list_k(j, n):
+            uq[n] = i
+            uk[n] = j
+            us[n] = kept(n)
+            return n + 1
+
+        return lax.fori_loop(lax.div(low, B), i + 1, list_k, n)
+
+    lax.fori_loop(0, 2, blank, 0)
+    units = lax.fori_loop(0, tiles, list_q, jnp.int32(2))
+    lax.fori_loop(units, units + 4, blank, 0)
+    pairs = lax.div(units + 1, 2) + 1
+
+    key_i = lax.broadcasted_iota(jnp.int32, (B, B), 0)
+    query_i = lax.broadcasted_iota(jnp.int32, (B, B), 1)
+    allowed = key_i <= query_i
+    causal[0] = jnp.full((B, B), jnp.inf, bf16)
+    causal[1] = jnp.where(allowed, jnp.inf, 0.0).astype(bf16)
+    probs[0] = jnp.zeros_like(probs[0])
+    for ref in (ds, qn, kn, g_qkv, g_out, g_up, g_down, g_norm, cot_s, heads_s, second_s, low_s, hidden_s, pre_s):
+        ref[...] = jnp.zeros_like(ref)
+
+    load[0].wait()
     for h in range(n_head):
-        qkv_h = jnp.concatenate([w_ref[h, d].astype(f32) for d in range(n_dp)], axis=0)
-        stage[...] = qkv_h
-        rp = w_ref.shape[2]
+        stage[...] = jnp.concatenate([w_ref[h, d].astype(f32) for d in range(n_dp)], axis=0)
         pick = lambda lo, n: jnp.concatenate(
             [stage[d * rp + lo : d * rp + lo + n] for d in range(n_dp)], axis=0
         )
         q = pick(0, rd)
         wqkv_t[h] = q.T[: 3 * HD].astype(bf16)
-        wqkv[:, h * 128 : (h + 1) * 128] = q.astype(bf16)
+        wqkv[:, h * 3 * HD : (h + 1) * 3 * HD] = q[:, : 3 * HD].astype(bf16)
         u = pick(rd, rd)
         wup[:, h * 128 : (h + 1) * 128] = u.astype(bf16)
         wup_t[h * 128 : (h + 1) * 128] = u.T.astype(bf16)
@@ -143,60 +222,18 @@
     wo = g_out[...]
     wout[...] = wo.astype(bf16)
     wout_t[...] = wo.T.astype(bf16)
+    g_out[...] = jnp.zeros_like(g_out)
     gain1, shift1 = gains[:, 0:1], gains[:, 1:2]
     gain2, shift2 = gains[:, 2:3], gains[:, 3:4]
 
-    starts, ends = [], []
-    at = jnp.int32(0)
-    for s in range(lengths.shape[1]):
-        starts.append(at)
-        at = at + lengths[row, s]
-        ends.append(at)
-    place = lax.broadcasted_iota(jnp.int32, (8, B), 0)
-    start_v = jnp.zeros((8, B), jnp.int32)
-    end_v = jnp.zeros((8, B), jnp.int32)
-    for s in range(8):
-        start_v = jnp.where(place == s, starts[s], start_v)
-        end_v = jnp.where(place == s, ends[s], end_v)
-    uq[0] = 0
-    uk[0] = 0
-    us[0] = 0
-
-    def list_q(i, n):
-        low = jnp.int32(0)
-        for s in range(1, 8):
-            low = jnp.where(starts[s] <= i * B, starts[s], low)
-
-        def list_k(j, n):
-            uq[n] = i
-            uk[n] = j
-            us[n] = jnp.minimum(n, CAP + 1)
-            return n + 1
-
-        return lax.fori_loop(lax.div(low, B), i + 1, list_k, n)
-
-    units = lax.fori_loop(0, tiles, list_q, jnp.int32(1))
-    uq[units] = 0
-    uk[units] = 0
-    us[units] = 0
-
-    key_i = lax.broadcasted_iota(jnp.int32, (B, B), 0)
-    query_i = lax.broadcasted_iota(jnp.int32, (B, B), 1)
-    allowed = key_i <= query_i
-    causal[0] = jnp.full((B, B), jnp.inf, bf16)
-    causal[1] = jnp.where(allowed, jnp.inf, 0.0).astype(bf16)
-    probs[0] = jnp.zeros_like(probs[0])
-    ds[...] = jnp.zeros_like(ds)
-    qn[...] = jnp.zeros_like(qn)
-    kn[...] = jnp.zeros_like(kn)
-    for ref in (acc, dk_acc, dv_acc, g_qkv, g_out, g_up, g_down, g_norm):
-        ref[...] = jnp.zeros_like(ref)
-
-    def project(i, carry):
+    def project(p, half):
+        i = 2 * p + half
         x = tokens[pl.ds(pl.multiple_of(i * B, B), B), :].astype(f32).T
+        yield
         n1, _ = stats(x)
         f = (n1 * gain1 + shift1).astype(bf16)
-        first[i] = f
+        first[p, :, half * B : (half + 1) * B] = f
+        yield
         where_t = i * B + lax.broadcasted_iota(jnp.int32, (8, B), 1)
         inside = ((where_t >= start_v) & (where_t < end_v)).astype(f32)
         penalty = (1.0 - inside) * -BIG
@@ -205,8 +242,9 @@
         zeros16 = jnp.zeros((16, B), f32)
         for h in range(HEADS):
             packed = mm(wqkv_t[h], f).astype(bf16)
+            yield
             pf = packed.astype(f32)
-            q = (pf[:HD] * QSCALE).astype(bf16).astype(f32)
+            q = pf[:HD]
             k = pf[HD : 2 * HD]
             v = pf[2 * HD :]
             qn[h] = jnp.maximum(qn[h], jnp.sum(q * q, axis=0, keepdims=True))
@@ -216,9 +254,13 @@
             vf[h, i] = jnp.concatenate([v, ones8, zeros8], axis=0).astype(bf16)
             kt[h, i] = jnp.concatenate([k, inside, ones8, zeros16], axis=0).T.astype(bf16)
             vt[h, i] = jnp.concatenate([v, ones8, zeros8, zeros16], axis=0).T.astype(bf16)
-        return carry
-
-    lax.fori_loop(0, tiles, project, 0)
+            acc[h, i] = jnp.zeros_like(acc[h, i])
+            dk_acc[h, i] = jnp.zeros_like(dk_acc[h, i])
+            dv_acc[h, i] = jnp.zeros_like(dv_acc[h, i])
+            yield
+
+    load[1].wait()
+    together(project, tiles)
 
     bound = jnp.float32(0.0)
     for h in range(HEADS):
@@ -227,7 +269,7 @@
     def scores(h, i, j):
         return mm(kt[h, j], qf[h, i])
 
-    @pl.when(jnp.logical_not(bound <= LIMIT * LIMIT))
+    @pl.when(jnp.logical_not(bound * SCALE**2 <= LIMIT * LIMIT))
     def _():
         bounds[...] = jnp.full_like(bounds, MASKED)
 
@@ -239,7 +281,7 @@
                 bounds[h, i] = jnp.maximum(bounds[h, i], jnp.max(s, axis=0, keepdims=True))
             return carry
 
-        lax.fori_loop(1, units, top, 0)
+        lax.fori_loop(2, units, top, 0)
 
         def shift(i, carry):
             for h in range(HEADS):
@@ -256,48 +298,76 @@
         i, j = uq[t], uk[t]
         cut = causal[jnp.where(i == j, 1, 0)]
         for h in range(HEADS):
-            probs[slot, h] = jnp.minimum(jnp.exp2(scores(h, i, j)).astype(bf16), cut)
-
-    def forward(t, carry):
-        i, j, slot = uq[t - 1], uk[t - 1], jnp.minimum(t - 1, CAP + 1)
-        for h in range(HEADS):
-            acc[h, i] += mm(vf[h, j, : HD + 8], probs[slot, h])
-        weigh(t, jnp.minimum(t, CAP + 1))
+            probs[slot, h] = jnp.minimum(jnp.exp2(scores(h, i, j) * SCALE).astype(bf16), cut)
+
+    def forward(p, carry):
+        for t in (2 * p - 2, 2 * p - 1):
+            i, j, slot = uq[t], uk[t], us[t]
+            for h in range(HEADS):
+                acc[h, i] += mm(vf[h, j, : HD + 8], probs[slot, h])
+        for t in (2 * p, 2 * p + 1):
+            weigh(t, kept(t))
         return carry
 
-    lax.fori_loop(1, units + 1, forward, 0)
-
-    def feed(i, carry):
+    lax.fori_loop(1, pairs, forward, 0)
+
+    def feed_grads():
+        g_down[...] += mm_nt(cot_s[...], hidden_s[...])
+        g_up[...] += mm_nt(second_s[...], pre_s[...])
+        g_out[...] += mm_nt(heads_s[...], low_s[...])
+
+    def write_tile(p, half, hbm):
+        i = 2 * p + half
         at = pl.ds(pl.multiple_of(i * B, B), B)
+        return pltpu.make_async_copy(result.at[at], hbm.at[at], stores.at[i])
+
+    def feed(p, half):
+        i = 2 * p + half
+        at = pl.ds(pl.multiple_of(i * B, B), B)
+        lanes = slice(half * B, (half + 1) * B)
+        if half == 0:
+            feed_grads()
         outs, inv = [], []
         for h in range(HEADS):
             r = 1.0 / acc[h, i, HD : HD + 1]
             inv.append(r)
             outs.append(acc[h, i, :HD] * r)
+            acc[h, i] = jnp.zeros_like(acc[h, i])
         heads = jnp.concatenate(outs, axis=0).astype(bf16)
         x = tokens[at, :].astype(f32).T
+        c32 = cot[at, :].astype(f32).T
+        c16 = c32.astype(bf16)
+        yield
         resid = x + mm(wout_t[...], heads)
+        yield
         n2, rate2 = stats(resid)
         second = (n2 * gain2 + shift2).astype(bf16)
-        c32 = cot[at, :].astype(f32).T
-        c16 = c32.astype(bf16)
-        pre = mm(wup_t[...], second)
-        back = mm(wdown_t[...], c16)
-        cdf = 0.5 * (1.0 + lax.erf(pre * (0.5**0.5)))
-        pdf = jnp.exp(-0.5 * pre * pre) * (1.0 / math.sqrt(2.0 * math.pi))
-        hidden = (pre * cdf).astype(bf16)
-        pre_grad = (back * (cdf + pre * pdf)).astype(bf16)
-        mixed[at, :] = (resid + mm(wdown[...], hidden)).T.astype(bf16)
-        g_down[...] += mm_nt(c16, hidden)
-        g_up[...] += mm_nt(second, pre_grad)
-        second_in = mm(wup[...], pre_grad)
+        yield
+        heads_s[:, lanes] = heads
+        cot_s[:, lanes] = c16
+        second_s[:, lanes] = second
+        for c in range(0, FF, 128):
+            rows = slice(c, c + 128)
+            pre = mm(wup_t[rows], second)
+            back = mm(wdown_t[rows], c16)
+            yield
+            cdf = 0.5 * (1.0 + lax.erf(pre * (0.5**0.5)))
+            pdf = jnp.exp(-0.5 * pre * pre) * (1.0 / math.sqrt(2.0 * math.pi))
+            hidden_s[rows, lanes] = (pre * cdf).astype(bf16)
+            pre_s[rows, lanes] = (back * (cdf + pre * pdf)).astype(bf16)
+            yield
+        second_in = mm(wup[...], pre_s[:, lanes])
+        yield
+        result[at, :] = (resid + mm(wdown[...], hidden_s[:, lanes])).T.astype(bf16)
         g_norm[2] += lane_fold(second_in * n2)
         g_norm[3] += lane_fold(second_in)
         rg = c32 + norm_back(second_in, n2, rate2, gain2)
+        low = rg.astype(bf16)
+        yield
+        hg = mm(wout[...], low).astype(bf16).astype(f32)
         resid_grad[i] = rg
-        low = rg.astype(bf16)
-        g_out[...] += mm_nt(heads, low)
-        hg = mm(wout[...], low).astype(bf16).astype(f32)
+        low_s[:, lanes] = low
+        yield
         zeros16 = jnp.zeros((16, B), f32)
         r8 = lax.broadcasted_iota(jnp.int32, (16, B), 0)
         for h in range(HEADS):
@@ -306,47 +376,64 @@
             one, two, three = split3(-delta)
             extra = jnp.where(r8 == 0, one, jnp.where(r8 == 1, two, jnp.where(r8 == 2, three, 0.0)))
             dof[h, i] = jnp.concatenate([do, extra, zeros16], axis=0).astype(bf16)
+        write_tile(p, half, mixed_hbm).start()
+
+    load[2].wait()
+    together(feed, tiles)
+    feed_grads()
+
+    def backward(p, carry):
+        for t in (2 * p, 2 * p + 1):
+            pl.when(us[t] > CAP)(lambda: weigh(t, us[t]))
+        for s, t in enumerate((2 * p - 2, 2 * p - 1)):
+            i, j = uq[t], uk[t]
+            for h in range(HEADS):
+                sg = ds[s, h]
+                acc[h, i, :HD] += mm(kf[h, j], sg)
+                dk_acc[h, j] += mm_nt(qf[h, i, :HD], sg)
+        for s, t in enumerate((2 * p, 2 * p + 1)):
+            i, j, slot = uq[t], uk[t], us[t]
+            for h in range(HEADS):
+                w = probs[slot, h]
+                pg = mm(vt[h, j], dof[h, i])
+                ds[s, h] = (w.astype(f32) * pg).astype(bf16)
+                dv_acc[h, j] += mm_nt(dof[h, i, :HD], w)
         return carry
 
-    lax.fori_loop(0, tiles, feed, 0)
-    acc[...] = jnp.zeros_like(acc)
-
-    def backward(t, carry):
-        pl.when(us[t] > CAP)(lambda: weigh(t, us[t]))
-        i, j = uq[t - 1], uk[t - 1]
-        old = lax.rem(t - 1, 2)
-        for h in range(HEADS):
-            sg = ds[old, h]
-            acc[h, i, :HD] += mm(kf[h, j], sg)
-            dk_acc[h, j] += mm_nt(qf[h, i, :HD], sg)
-        i, j, slot = uq[t], uk[t], us[t]
-        new = lax.rem(t, 2)
-        for h in range(HEADS):
-            p = probs[slot, h]
-            pg = mm(vt[h, j], dof[h, i])
-            ds[new, h] = (p.astype(f32) * pg).astype(bf16)
-            dv_acc[h, j] += mm_nt(dof[h, i, :HD], p)
+    lax.fori_loop(1, pairs, backward, 0)
+
+    def wait_tile(i, carry):
+        at = pl.ds(pl.multiple_of(i * B, B), B)
+        pltpu.make_async_copy(result.at[at], mixed_hbm.at[at], stores.at[i]).wait()
         return carry
 
-    lax.fori_loop(1, units + 1, backward, 0)
-
-    def finish(i, carry):
+    lax.fori_loop(0, tiles, wait_tile, 0)
+
+    def finish(p, half):
+        i = 2 * p + half
         at = pl.ds(pl.multiple_of(i * B, B), B)
+        lanes = slice(half * B, (half + 1) * B)
         rows = []
         for h in range(HEADS):
-            rows += [acc[h, i, :HD] * HD**-0.5, dk_acc[h, i] * LN2, dv_acc[h, i], jnp.zeros((HD, B), f32)]
+            rows += [acc[h, i, :HD] * HD**-0.5, dk_acc[h, i] * HD**-0.5, dv_acc[h, i]]
         packed_grad = jnp.concatenate(rows, axis=0).astype(bf16)
-        g_qkv[...] += mm_nt(first[i], packed_grad)
+        hidden_s[: 3 * D, lanes] = packed_grad
+        yield
         first_in = mm(wqkv[...], packed_grad)
+        if half == 1:
+            g_qkv[...] += mm_nt(first[p], hidden_s[: 3 * D, :])
         x = tokens[at, :].astype(f32).T
+        yield
         n1, rate1 = stats(x)
+        yield
         g_norm[0] += lane_fold(first_in * n1)
         g_norm[1] += lane_fold(first_in)
         out = resid_grad[i] + norm_back(first_in, n1, rate1, gain1)
-        igrad[at, :] = out.T.astype(bf16)
-        return carry
-
-    lax.fori_loop(0, tiles, finish, 0)
+        yield
+        result[at, :] = out.T.astype(bf16)
+        write_tile(p, half, igrad_hbm).start()
+
+    together(finish, tiles)
 
     lane = lax.broadcasted_iota(jnp.int32, (D, 128), 1)
     norm = jnp.zeros((D, 128), f32)
@@ -356,29 +443,47 @@
     g_stage[...] = jnp.zeros_like(g_stage)
     for h in range(n_head):
         cols = slice(h * 128, (h + 1) * 128)
+        qkv = g_qkv[:, h * 3 * HD : (h + 1) * 3 * HD]
         for d in range(n_dp):
             rows = slice(d * rd, (d + 1) * rd)
             at = (d * n_head + h) * ro
-            g_stage[0:rd] = g_qkv[rows, cols]
+            g_stage[0:rd, : 3 * HD] = qkv[rows]
             g_stage[rd : 2 * rd] = g_up[rows, cols]
             g_stage[2 * rd : 3 * rd] = g_down[rows, cols]
             g_stage[3 * rd : 3 * rd + ro] = g_out[at : at + ro]
             g_stage[3 * rd + ro : 3 * rd + 2 * ro] = gains[at : at + ro]
             grads[h, d] = g_stage[...].astype(bf16)
+    out = pltpu.make_async_copy(grads, grads_hbm, loads.at[0])
+    out.start()
+
+    def wait_last(i, carry):
+        at = pl.ds(pl.multiple_of(i * B, B), B)
+        pltpu.make_async_copy(result.at[at], igrad_hbm.at[at], stores.at[i]).wait()
+        return carry
+
+    lax.fori_loop(0, tiles, wait_last, 0)
+    out.wait()
 
 
 def layer(lengths, weights, tokens, cot, rd, ro):
     n_head, n_dp, rp = weights.shape[:3]
     tiles = tokens.shape[0] // B
-    listed = tiles * (MAX_LEN // B + 1) + 2
+    listed = tiles * (MAX_LEN // B + 1) + 8
     vmem = lambda shape, dtype: pltpu.VMEM(shape, dtype)
     scratch = [
         pltpu.SMEM((listed,), jnp.int32),
         pltpu.SMEM((listed,), jnp.int32),
         pltpu.SMEM((listed,), jnp.int32),
+        vmem(weights.shape, bf16),
+        vmem(tokens.shape, bf16),
+        vmem(tokens.shape, bf16),
+        vmem(tokens.shape, bf16),
+        vmem((n_head, n_dp, rp, 128), bf16),
+        pltpu.SemaphoreType.DMA((3,)),
+        pltpu.SemaphoreType.DMA((tiles,)),
         vmem((HEADS, tiles, 1, B), f32),
         vmem((HEADS, 3 * HD, D), bf16),
-        vmem((D, HEADS * 128), bf16),
+        vmem((D, 3 * D), bf16),
         vmem((D, D), bf16),
         vmem((D, D), bf16),
         vmem((D, FF), bf16),
@@ -393,24 +498,29 @@
         vmem((HEADS, tiles, B, 64), bf16),
         vmem((HEADS, tiles, B, 64), bf16),
         vmem((HEADS, tiles, 64, B), bf16),
-        vmem((CAP + 2, HEADS, B, B), bf16),
+        vmem((CAP + 3, HEADS, B, B), bf16),
         vmem((2, HEADS, B, B), bf16),
         vmem((HEADS, tiles, HD + 8, B), f32),
         vmem((HEADS, tiles, HD, B), f32),
         vmem((HEADS, tiles, HD, B), f32),
         vmem((tiles, D, B), f32),
-        vmem((tiles, D, B), bf16),
+        vmem((tiles // 2, D, WIDE), bf16),
+        vmem((D, WIDE), bf16),
+        vmem((D, WIDE), bf16),
+        vmem((D, WIDE), bf16),
+        vmem((D, WIDE), bf16),
+        vmem((FF, WIDE), bf16),
+        vmem((FF, WIDE), bf16),
         vmem((2, B, B), bf16),
         vmem((HEADS, 1, B), f32),
         vmem((HEADS, 1, B), f32),
-        vmem((D, HEADS * 128), f32),
+        vmem((D, 3 * D), f32),
         vmem((D, D), f32),
         vmem((D, FF), f32),
         vmem((D, FF), f32),
         vmem((4, D, 128), f32),
         vmem((rp, 128), f32),
     ]
-    whole = pl.BlockSpec(memory_space=pltpu.VMEM)
     return pl.pallas_call(
         functools.partial(layer_kernel, rd, ro),
         out_shape=(
@@ -418,10 +528,10 @@
             jax.ShapeDtypeStruct(tokens.shape, bf16),
             jax.ShapeDtypeStruct((n_head, n_dp, rp, 128), bf16),
         ),
-        in_specs=[pl.BlockSpec(memory_space=pltpu.SMEM), whole, whole, whole],
-        out_specs=(whole, whole, whole),
+        in_specs=[pl.BlockSpec(memory_space=pltpu.SMEM), ANY, ANY, ANY],
+        out_specs=(ANY, ANY, ANY),
         scratch_shapes=scratch,
-        compiler_params=pltpu.CompilerParams(vmem_limit_bytes=62 * 1024 * 1024),
+        compiler_params=pltpu.CompilerParams(vmem_limit_bytes=63 * 1024 * 1024),
     )(lengths, weights, tokens, cot)
 
 
@@ -525,10 +635,6 @@
         copy.wait_send()
 
 
-ANY = pl.BlockSpec(memory_space=pl.ANY)
-WHOLE = pl.BlockSpec(memory_space=pltpu.VMEM)
-
-
 def copies_of(axes, groups):
     return sum(math.prod(axes[a][2] for a in group) - 1 for group in groups)
 
@@ -550,7 +656,7 @@
             pltpu.SemaphoreType.DMA((copies,)),
         ],
         compiler_params=pltpu.CompilerParams(
-            collective_id=cid, has_side_effects=True, vmem_limit_bytes=32 * 1024 * 1024
+            collective_id=cid, has_side_effects=True, vmem_limit_bytes=62 * 1024 * 1024
         ),
     )(*masters)
 
@@ -644,7 +750,7 @@
             pltpu.SemaphoreType.DMA((copies,)),
         ],
         compiler_params=pltpu.CompilerParams(
-            collective_id=cid, has_side_effects=True, vmem_limit_bytes=32 * 1024 * 1024
+            collective_id=cid, has_side_effects=True, vmem_limit_bytes=65228 * 1024
         ),
     )(grads)
 
@@ -684,7 +790,6 @@
 
 
 def update(red, sq, params):
-    whole = pl.BlockSpec(memory_space=pltpu.VMEM)
     like = lambda p, dtype: jax.ShapeDtypeStruct(p.shape, dtype)
     shapes = [jax.ShapeDtypeStruct((1, 1), f32)]
     shapes += [like(p, f32) for p in params[:5] for _ in range(3)]
@@ -693,8 +798,8 @@
     return pl.pallas_call(
         update_kernel,
         out_shape=shapes,
-        in_specs=[whole] * 17,
-        out_specs=[whole] * len(shapes),
+        in_specs=[WHOLE] * 17,
+        out_specs=[WHOLE] * len(shapes),
         compiler_params=pltpu.CompilerParams(vmem_limit_bytes=32 * 1024 * 1024),
     )(red, sq, *params)
 

time: 122 us -> 103 us (0.84)
  Pallas kernels: 115 us -> 99.9 us
  local copies, waits for them, and re-layouts: 5.9 us -> 1.38 us
    pallas_call x1, Pallas kernels: 81.5 us -> 63 us  [layer(): pl.pallas_call(functools.partial(layer_kernel, rd, ro), out_shape=(jax.Sh...]
    unnamed x44 -> x34, local copies, waits for them, and re-layouts: 5.9 us -> 1.38 us
    pallas_call x1, Pallas kernels: 18.1 us -> 20.8 us  [scatter(): pl.pallas_call(functools.partial(scatter_kernel, axes, groups, sums), out...]
where the time goes in v3:
time: 103 us; the launch traced here: 102 us
  Pallas kernels  99.9 us (97%)
  local copies, waits for them, and re-layouts  1.38 us (1%)
    pallas_call x1, Pallas kernels, layer(): pl.pallas_call(functools.partial(layer_kernel, rd, ro), out_shape=(jax.Sh...  63 us
    pallas_call x1, Pallas kernels, scatter(): pl.pallas_call(functools.partial(scatter_kernel, axes, groups, sums), out...  20.8 us
    pallas_call x1, Pallas kernels, gather(): pl.pallas_call(functools.partial(gather_kernel, axes, groups), out_shape=...  15.2 us

profile of v3, /device:TPU:0, one launch (start us, length us, event | category | flops | bytes accessed | tf_op | source)
XLA Modules:
  0.0 102.2 jit_solution(2001229812637984144)
XLA Ops:
  0.7 15.2 %shard_map.393 = bf16[2,2,4,2,64,128]{5,4,3,2,1,0:T(8,128)(2,1)} custom-call(f32[16,96]{1,0:T(8,128)} %refs_0_.3, f32[4,128]{1,0:T(4,128)} %refs_1_.3, f32[16,128]{1,0:T(8,128)} %refs_2_.3, f32[16,128]{1,0:T(8,128)} %refs_3_.3, f32[4,4]{1,0:T(4,128)} %refs_4_.3), custom_call_target="tpu_custom_call" | custom-call | tf_op jit(solution)/shard_map/pallas_call | solution.py:645
  15.9 63.0 %shard_map.394 = (bf16[4096,128]{1,0:T(8,128)(2,1)}, bf16[4096,128]{1,0:T(8,128)(2,1)}, bf16[4,8,64,128]{3,2,1,0:T(8,128)(2,1)}) custom-call(s32[4,8]{1,0:T(4,128)} %lengths.1, bf16[4,8,64,128]{3,2,1,0:T(8,128)(2,1)} %bitcast.3, bf16[4096,128]{1,0:T(8,128)(2,1)} %tokens_hbm.1, bf16[4096,128]{1,0:T(8,128)(2,1)} %cot_hbm.1), custom_call_target="tpu_custom_call" | custom-call | tf_op jit(solution)/shard_map/pallas_call | solution.py:524
  79.0 0.0 copy-start
  79.0 0.0 copy-start.1
  79.0 0.0 copy-start.2
  79.0 0.0 copy-start.5
  79.0 0.0 copy-start.6
  79.0 0.0 copy-start.7
  79.0 0.0 copy-start.8
  79.0 0.0 copy-start.9
  79.1 0.0 copy-start.10
  79.1 0.0 copy-start.11
  79.1 0.0 copy-start.12
  79.1 0.0 copy-start.13
  79.1 0.0 copy-start.14
  79.1 0.0 copy-start.15
  79.1 20.8 %shard_map.395 = (f32[64,128]{1,0:T(8,128)}, f32[1,128]{1,0:T(1,128)}) custom-call(bf16[2,2,4,2,64,128]{5,4,3,2,1,0:T(8,128)(2,1)} %bitcast.4), custom_call_target="tpu_custom_call" | custom-call | tf_op jit(solution)/shard_map/pallas_call | solution.py:738
  99.9 0.0 copy-start.4
  99.9 0.0 copy-start.16
  99.9 0.0 copy-done
  99.9 0.0 copy-done.1
  100.0 0.0 copy-done.2
  100.0 0.0 copy-done.5
  100.0 0.0 copy-done.6
  100.0 0.0 copy-done.7
  100.0 0.0 copy-done.8
  100.0 0.0 copy-done.9
  100.0 0.0 copy-done.10
  100.0 0.0 copy-done.11
  100.1 0.5 copy-done.4
  100.6 0.8 copy-done.3
  101.4 0.8 shard_map.396
  (6 shorter events, 0.0 us)
Async XLA Ops:
  79.0 21.0 %copy-start = (f32[16,96]{1,0:T(8,128)S(1)}, f32[16,96]{1,0:T(8,128)}, u32[]{:S(2)}) copy-start(f32[16,96]{1,0:T(8,128)} %refs_0_.3) | copy-start | bytes 18436
  79.0 21.0 %copy-start.1 = (f32[16,128]{1,0:T(8,128)S(1)}, f32[16,128]{1,0:T(8,128)}, u32[]{:S(2)}) copy-start(f32[16,128]{1,0:T(8,128)} %refs_2_.3) | copy-start | bytes 24580
  79.0 21.0 %copy-start.2 = (f32[16,128]{1,0:T(8,128)S(1)}, f32[16,128]{1,0:T(8,128)}, u32[]{:S(2)}) copy-start(f32[16,128]{1,0:T(8,128)} %refs_3_.3) | copy-start | bytes 24580
  79.0 21.0 %copy-start.5 = (f32[4,4]{1,0:T(4,128)S(1)}, f32[4,4]{1,0:T(4,128)}, u32[]{:S(2)}) copy-start(f32[4,4]{1,0:T(4,128)} %refs_4_.3) | copy-start | bytes 196
  79.0 21.0 %copy-start.6 = (f32[16,96]{1,0:T(8,128)S(1)}, f32[16,96]{1,0:T(8,128)}, u32[]{:S(2)}) copy-start(f32[16,96]{1,0:T(8,128)} %refs_5_.1) | copy-start | bytes 18436
  79.0 21.0 %copy-start.7 = (f32[16,128]{1,0:T(8,128)S(1)}, f32[16,128]{1,0:T(8,128)}, u32[]{:S(2)}) copy-start(f32[16,128]{1,0:T(8,128)} %refs_7_.1) | copy-start | bytes 24580
  79.0 21.0 %copy-start.8 = (f32[16,128]{1,0:T(8,128)S(1)}, f32[16,128]{1,0:T(8,128)}, u32[]{:S(2)}) copy-start(f32[16,128]{1,0:T(8,128)} %refs_8_.1) | copy-start | bytes 24580
  79.0 21.0 %copy-start.9 = (f32[16,96]{1,0:T(8,128)S(1)}, f32[16,96]{1,0:T(8,128)}, u32[]{:S(2)}) copy-start(f32[16,96]{1,0:T(8,128)} %refs_10_.1) | copy-start | bytes 18436
  79.1 21.0 %copy-start.10 = (f32[16,128]{1,0:T(8,128)S(1)}, f32[16,128]{1,0:T(8,128)}, u32[]{:S(2)}) copy-start(f32[16,128]{1,0:T(8,128)} %refs_12_.1) | copy-start | bytes 24580
  79.1 21.0 %copy-start.11 = (f32[16,128]{1,0:T(8,128)S(1)}, f32[16,128]{1,0:T(8,128)}, u32[]{:S(2)}) copy-start(f32[16,128]{1,0:T(8,128)} %refs_13_.1) | copy-start | bytes 24580
  79.1 21.0 %copy-start.12 = (f32[4,128]{1,0:T(4,128)S(1)}, f32[4,128]{1,0:T(4,128)}, u32[]{:S(2)}) copy-start(f32[4,128]{1,0:T(4,128)} %refs_6_.1) | copy-start | bytes 6148
  79.1 21.0 %copy-start.13 = (f32[4,4]{1,0:T(4,128)S(1)}, f32[4,4]{1,0:T(4,128)}, u32[]{:S(2)}) copy-start(f32[4,4]{1,0:T(4,128)} %refs_9_.1) | copy-start | bytes 196
  79.1 21.0 %copy-start.14 = (f32[4,128]{1,0:T(4,128)S(1)}, f32[4,128]{1,0:T(4,128)}, u32[]{:S(2)}) copy-start(f32[4,128]{1,0:T(4,128)} %refs_11_.1) | copy-start | bytes 6148
  79.1 21.0 %copy-start.15 = (f32[4,4]{1,0:T(4,128)S(1)}, f32[4,4]{1,0:T(4,128)}, u32[]{:S(2)}) copy-start(f32[4,4]{1,0:T(4,128)} %refs_14_.1) | copy-start | bytes 196
  99.9 0.7 copy-start.4
  99.9 0.7 copy-start.16
  100.6 0.8 copy-start.3

commit v4 on v3

--- a/solution.py
+++ b/solution.py
@@ -22,8 +22,11 @@
 D = 128
 FF = 512
 B = 256
-CAP = 50
-WIDE = 2 * B
+CAP = 46
+CHUNK = 128
+GROUP = 2
+SIDE = 4
+WIDE = SIDE * B
 BIG = 2.0**100
 LIMIT = 88.0
 MASKED = -1e30
@@ -31,7 +34,7 @@
 f32 = jnp.float32
 bf16 = jnp.bfloat16
 MESH = pl.DeviceIdType.MESH
-ANY = pl.BlockSpec(memory_space=pl.ANY)
+HBM = pl.BlockSpec(memory_space=pltpu.HBM)
 WHOLE = pl.BlockSpec(memory_space=pltpu.VMEM)
 
 
@@ -73,12 +76,12 @@
 
 def together(steps, tiles):
     def pair(p, carry):
-        running = [steps(p, half) for half in range(2)]
+        running = [steps(p, half) for half in range(SIDE)]
         while running:
             running = [r for r in running if next(r, "done") != "done"]
         return carry
 
-    lax.fori_loop(0, tiles // 2, pair, 0)
+    lax.fori_loop(0, tiles // SIDE, pair, 0)
 
 
 def layer_kernel(
@@ -119,7 +122,8 @@
     vt,
     dof,
     probs,
-    ds,
+    turn_a,
+    turn_b,
     acc,
     dk_acc,
     dv_acc,
@@ -165,7 +169,7 @@
         end_v = jnp.where(place == s, ends[s], end_v)
 
     def kept(t):
-        return jnp.where(t - 1 <= CAP, t - 1, CAP + 1 + lax.rem(t, 2))
+        return jnp.where(t - GROUP < CAP, t - GROUP + 1, CAP + 1 + lax.rem(t, GROUP))
 
     def blank(t, carry):
         uq[t] = 0
@@ -186,18 +190,19 @@
 
         return lax.fori_loop(lax.div(low, B), i + 1, list_k, n)
 
-    lax.fori_loop(0, 2, blank, 0)
-    units = lax.fori_loop(0, tiles, list_q, jnp.int32(2))
-    lax.fori_loop(units, units + 4, blank, 0)
-    pairs = lax.div(units + 1, 2) + 1
+    lax.fori_loop(0, GROUP, blank, 0)
+    units = lax.fori_loop(0, tiles, list_q, jnp.int32(GROUP))
+    lax.fori_loop(units, units + 2 * GROUP, blank, 0)
+    steps = lax.div(units, GROUP) + 1
 
     key_i = lax.broadcasted_iota(jnp.int32, (B, B), 0)
     query_i = lax.broadcasted_iota(jnp.int32, (B, B), 1)
     allowed = key_i <= query_i
     causal[0] = jnp.full((B, B), jnp.inf, bf16)
     causal[1] = jnp.where(allowed, jnp.inf, 0.0).astype(bf16)
+    causal[2] = jnp.zeros((B, B), bf16)
     probs[0] = jnp.zeros_like(probs[0])
-    for ref in (ds, qn, kn, g_qkv, g_out, g_up, g_down, g_norm, cot_s, heads_s, second_s, low_s, hidden_s, pre_s):
+    for ref in (qn, kn, g_qkv, g_out, g_up, g_down, g_norm, cot_s, heads_s, second_s, low_s, hidden_s, pre_s):
         ref[...] = jnp.zeros_like(ref)
 
     load[0].wait()
@@ -227,7 +232,7 @@
     gain2, shift2 = gains[:, 2:3], gains[:, 3:4]
 
     def project(p, half):
-        i = 2 * p + half
+        i = SIDE * p + half
         x = tokens[pl.ds(pl.multiple_of(i * B, B), B), :].astype(f32).T
         yield
         n1, _ = stats(x)
@@ -236,24 +241,26 @@
         yield
         where_t = i * B + lax.broadcasted_iota(jnp.int32, (8, B), 1)
         inside = ((where_t >= start_v) & (where_t < end_v)).astype(f32)
-        penalty = (1.0 - inside) * -BIG
         zeros8 = jnp.zeros((8, B), f32)
         ones8 = jnp.ones((8, B), f32)
-        zeros16 = jnp.zeros((16, B), f32)
+        key_side = jnp.concatenate([inside, ones8], axis=0).astype(bf16)
+        query_side = jnp.concatenate([(1.0 - inside) * -BIG, zeros8], axis=0).astype(bf16)
+        value_side = jnp.concatenate([ones8, zeros8], axis=0).astype(bf16)
         for h in range(HEADS):
             packed = mm(wqkv_t[h], f).astype(bf16)
             yield
-            pf = packed.astype(f32)
-            q = pf[:HD]
-            k = pf[HD : 2 * HD]
-            v = pf[2 * HD :]
-            qn[h] = jnp.maximum(qn[h], jnp.sum(q * q, axis=0, keepdims=True))
-            kn[h] = jnp.maximum(kn[h], jnp.sum(k * k, axis=0, keepdims=True))
-            qf[h, i] = jnp.concatenate([q, penalty, zeros8, zeros16], axis=0).astype(bf16)
-            kf[h, i] = packed[HD : 2 * HD]
-            vf[h, i] = jnp.concatenate([v, ones8, zeros8], axis=0).astype(bf16)
-            kt[h, i] = jnp.concatenate([k, inside, ones8, zeros16], axis=0).T.astype(bf16)
-            vt[h, i] = jnp.concatenate([v, ones8, zeros8, zeros16], axis=0).T.astype(bf16)
+            q, k, v = (packed[n * HD : (n + 1) * HD] for n in range(3))
+            squares = packed.astype(f32)
+            squares = squares * squares
+            qn[h] = jnp.maximum(qn[h], jnp.sum(squares[:HD], axis=0, keepdims=True))
+            kn[h] = jnp.maximum(kn[h], jnp.sum(squares[HD : 2 * HD], axis=0, keepdims=True))
+            qf[h, i, :HD] = q
+            qf[h, i, HD:] = query_side
+            kf[h, i] = k
+            vf[h, i, :HD] = v
+            vf[h, i, HD:] = value_side
+            kt[h, i] = jnp.concatenate([k, key_side], axis=0).T
+            vt[h, i] = jnp.concatenate([v, value_side], axis=0).T
             acc[h, i] = jnp.zeros_like(acc[h, i])
             dk_acc[h, i] = jnp.zeros_like(dk_acc[h, i])
             dv_acc[h, i] = jnp.zeros_like(dv_acc[h, i])
@@ -281,7 +288,7 @@
                 bounds[h, i] = jnp.maximum(bounds[h, i], jnp.max(s, axis=0, keepdims=True))
             return carry
 
-        lax.fori_loop(2, units, top, 0)
+        lax.fori_loop(GROUP, units, top, 0)
 
         def shift(i, carry):
             for h in range(HEADS):
@@ -294,35 +301,40 @@
 
         lax.fori_loop(0, tiles, shift, 0)
 
-    def weigh(t, slot):
+    def weigh(t, slot, *kept_too):
         i, j = uq[t], uk[t]
-        cut = causal[jnp.where(i == j, 1, 0)]
+        cut = causal[jnp.where(t >= units, 2, jnp.where(i == j, 1, 0))]
         for h in range(HEADS):
-            probs[slot, h] = jnp.minimum(jnp.exp2(scores(h, i, j) * SCALE).astype(bf16), cut)
+            p = jnp.minimum(jnp.exp2(scores(h, i, j) * SCALE).astype(bf16), cut)
+            for ref in (probs.at[slot], *kept_too):
+                ref[h] = p
 
     def forward(p, carry):
-        for t in (2 * p - 2, 2 * p - 1):
-            i, j, slot = uq[t], uk[t], us[t]
+        for u in range(GROUP):
+            t = GROUP * p + u
+            weigh(t, kept(t), turns[u % 2])
+            i, j = uq[t - 1], uk[t - 1]
             for h in range(HEADS):
-                acc[h, i] += mm(vf[h, j, : HD + 8], probs[slot, h])
-        for t in (2 * p, 2 * p + 1):
-            weigh(t, kept(t))
+                acc[h, i] += mm(vf[h, j, : HD + 8], turns[1 - u % 2][h])
         return carry
 
-    lax.fori_loop(1, pairs, forward, 0)
+    turns = (turn_a, turn_b)
+    for ref in turns:
+        ref[...] = jnp.zeros_like(ref)
+    lax.fori_loop(1, steps, forward, 0)
 
     def feed_grads():
-        g_down[...] += mm_nt(cot_s[...], hidden_s[...])
-        g_up[...] += mm_nt(second_s[...], pre_s[...])
+        g_down[...] += mm_nt(hidden_s[...], cot_s[...])
+        g_up[...] += mm_nt(pre_s[...], second_s[...])
         g_out[...] += mm_nt(heads_s[...], low_s[...])
 
     def write_tile(p, half, hbm):
-        i = 2 * p + half
+        i = SIDE * p + half
         at = pl.ds(pl.multiple_of(i * B, B), B)
         return pltpu.make_async_copy(result.at[at], hbm.at[at], stores.at[i])
 
     def feed(p, half):
-        i = 2 * p + half
+        i = SIDE * p + half
         at = pl.ds(pl.multiple_of(i * B, B), B)
         lanes = slice(half * B, (half + 1) * B)
         if half == 0:
@@ -346,8 +358,8 @@
         heads_s[:, lanes] = heads
         cot_s[:, lanes] = c16
         second_s[:, lanes] = second
-        for c in range(0, FF, 128):
-            rows = slice(c, c + 128)
+        for c in range(0, FF, CHUNK):
+            rows = slice(c, c + CHUNK)
             pre = mm(wup_t[rows], second)
             back = mm(wdown_t[rows], c16)
             yield
@@ -368,14 +380,15 @@
         resid_grad[i] = rg
         low_s[:, lanes] = low
         yield
-        zeros16 = jnp.zeros((16, B), f32)
         r8 = lax.broadcasted_iota(jnp.int32, (16, B), 0)
         for h in range(HEADS):
-            do = (hg[h * HD : (h + 1) * HD] * inv[h]).astype(bf16).astype(f32)
+            do16 = (hg[h * HD : (h + 1) * HD] * inv[h]).astype(bf16)
+            do = do16.astype(f32)
             delta = jnp.sum(do * outs[h], axis=0, keepdims=True)
             one, two, three = split3(-delta)
             extra = jnp.where(r8 == 0, one, jnp.where(r8 == 1, two, jnp.where(r8 == 2, three, 0.0)))
-            dof[h, i] = jnp.concatenate([do, extra, zeros16], axis=0).astype(bf16)
+            dof[h, i, :HD] = do16
+            dof[h, i, HD:] = extra.astype(bf16)
         write_tile(p, half, mixed_hbm).start()
 
     load[2].wait()
@@ -383,24 +396,27 @@
     feed_grads()
 
     def backward(p, carry):
-        for t in (2 * p, 2 * p + 1):
+        for u in range(GROUP):
+            t = GROUP * p + u
             pl.when(us[t] > CAP)(lambda: weigh(t, us[t]))
-        for s, t in enumerate((2 * p - 2, 2 * p - 1)):
-            i, j = uq[t], uk[t]
-            for h in range(HEADS):
-                sg = ds[s, h]
-                acc[h, i, :HD] += mm(kf[h, j], sg)
-                dk_acc[h, j] += mm_nt(qf[h, i, :HD], sg)
-        for s, t in enumerate((2 * p, 2 * p + 1)):
+        for u in range(GROUP):
+            t = GROUP * p + u
             i, j, slot = uq[t], uk[t], us[t]
             for h in range(HEADS):
                 w = probs[slot, h]
                 pg = mm(vt[h, j], dof[h, i])
-                ds[s, h] = (w.astype(f32) * pg).astype(bf16)
+                turns[u % 2][h] = (w.astype(f32) * pg).astype(bf16)
                 dv_acc[h, j] += mm_nt(dof[h, i, :HD], w)
+            i, j = uq[t - 1], uk[t - 1]
+            for h in range(HEADS):
+                sg = turns[1 - u % 2][h]
+                acc[h, i, :HD] += mm(kf[h, j], sg)
+                dk_acc[h, j] += mm_nt(qf[h, i, :HD], sg)
         return carry
 
-    lax.fori_loop(1, pairs, backward, 0)
+    for ref in turns:
+        ref[...] = jnp.zeros_like(ref)
+    lax.fori_loop(1, steps, backward, 0)
 
     def wait_tile(i, carry):
         at = pl.ds(pl.multiple_of(i * B, B), B)
@@ -410,7 +426,7 @@
     lax.fori_loop(0, tiles, wait_tile, 0)
 
     def finish(p, half):
-        i = 2 * p + half
+        i = SIDE * p + half
         at = pl.ds(pl.multiple_of(i * B, B), B)
         lanes = slice(half * B, (half + 1) * B)
         rows = []
@@ -420,8 +436,8 @@
         hidden_s[: 3 * D, lanes] = packed_grad
         yield
         first_in = mm(wqkv[...], packed_grad)
-        if half == 1:
-            g_qkv[...] += mm_nt(first[p], hidden_s[: 3 * D, :])
+        if half == SIDE - 1:
+            g_qkv[...] += mm_nt(hidden_s[: 3 * D, :], first[p])
         x = tokens[at, :].astype(f32).T
         yield
         n1, rate1 = stats(x)
@@ -443,13 +459,14 @@
     g_stage[...] = jnp.zeros_like(g_stage)
     for h in range(n_head):
         cols = slice(h * 128, (h + 1) * 128)
-        qkv = g_qkv[:, h * 3 * HD : (h + 1) * 3 * HD]
+        qkv = g_qkv[h * 3 * HD : (h + 1) * 3 * HD].T
+        up, down = g_up[cols].T, g_down[cols].T
         for d in range(n_dp):
             rows = slice(d * rd, (d + 1) * rd)
             at = (d * n_head + h) * ro
             g_stage[0:rd, : 3 * HD] = qkv[rows]
-            g_stage[rd : 2 * rd] = g_up[rows, cols]
-            g_stage[2 * rd : 3 * rd] = g_down[rows, cols]
+            g_stage[rd : 2 * rd] = up[rows]
+            g_stage[2 * rd : 3 * rd] = down[rows]
             g_stage[3 * rd : 3 * rd + ro] = g_out[at : at + ro]
             g_stage[3 * rd + ro : 3 * rd + 2 * ro] = gains[at : at + ro]
             grads[h, d] = g_stage[...].astype(bf16)
@@ -468,7 +485,7 @@
 def layer(lengths, weights, tokens, cot, rd, ro):
     n_head, n_dp, rp = weights.shape[:3]
     tiles = tokens.shape[0] // B
-    listed = tiles * (MAX_LEN // B + 1) + 8
+    listed = tiles * (MAX_LEN // B + 1) + 3 * GROUP + 2
     vmem = lambda shape, dtype: pltpu.VMEM(shape, dtype)
     scratch = [
         pltpu.SMEM((listed,), jnp.int32),
@@ -492,32 +509,33 @@
         vmem((FF, D), bf16),
         vmem((D, 128), f32),
         vmem((n_dp * rp, 128), f32),
-        vmem((HEADS, tiles, 64, B), bf16),
+        vmem((HEADS, tiles, 48, B), bf16),
         vmem((HEADS, tiles, HD, B), bf16),
         vmem((HEADS, tiles, 48, B), bf16),
-        vmem((HEADS, tiles, B, 64), bf16),
-        vmem((HEADS, tiles, B, 64), bf16),
-        vmem((HEADS, tiles, 64, B), bf16),
-        vmem((CAP + 3, HEADS, B, B), bf16),
-        vmem((2, HEADS, B, B), bf16),
+        vmem((HEADS, tiles, B, 48), bf16),
+        vmem((HEADS, tiles, B, 48), bf16),
+        vmem((HEADS, tiles, 48, B), bf16),
+        vmem((CAP + 1 + GROUP, HEADS, B, B), bf16),
+        vmem((HEADS, B, B), bf16),
+        vmem((HEADS, B, B), bf16),
         vmem((HEADS, tiles, HD + 8, B), f32),
         vmem((HEADS, tiles, HD, B), f32),
         vmem((HEADS, tiles, HD, B), f32),
         vmem((tiles, D, B), f32),
-        vmem((tiles // 2, D, WIDE), bf16),
+        vmem((tiles // SIDE, D, WIDE), bf16),
         vmem((D, WIDE), bf16),
         vmem((D, WIDE), bf16),
         vmem((D, WIDE), bf16),
         vmem((D, WIDE), bf16),
         vmem((FF, WIDE), bf16),
         vmem((FF, WIDE), bf16),
-        vmem((2, B, B), bf16),
+        vmem((3, B, B), bf16),
         vmem((HEADS, 1, B), f32),
         vmem((HEADS, 1, B), f32),
-        vmem((D, 3 * D), f32),
+        vmem((3 * D, D), f32),
         vmem((D, D), f32),
-        vmem((D, FF), f32),
-        vmem((D, FF), f32),
+        vmem((FF, D), f32),
+        vmem((FF, D), f32),
         vmem((4, D, 128), f32),
         vmem((rp, 128), f32),
     ]
@@ -528,8 +546,8 @@
             jax.ShapeDtypeStruct(tokens.shape, bf16),
             jax.ShapeDtypeStruct((n_head, n_dp, rp, 128), bf16),
         ),
-        in_specs=[pl.BlockSpec(memory_space=pltpu.SMEM), ANY, ANY, ANY],
-        out_specs=(ANY, ANY, ANY),
+        in_specs=[pl.BlockSpec(memory_space=pltpu.SMEM), HBM, HBM, HBM],
+        out_specs=(HBM, HBM, HBM),
         scratch_shapes=scratch,
         compiler_params=pltpu.CompilerParams(vmem_limit_bytes=63 * 1024 * 1024),
     )(lengths, weights, tokens, cot)
@@ -537,15 +555,11 @@
 
 def factors(n_dp, n_head):
     if (n_dp, n_head) == (8, 4):
-        axes = (("head", 2, 2), ("head", 1, 2), ("dp", 2, 4), ("dp", 1, 2))
-        return axes, ((2,), (0, 3), (1,)), ((1,), (0, 3), (2,)), ((1,), (0, 2, 3))
-    axes, left = [("head", 1, n_head)], n_dp
-    while left > 1:
-        size = 4 if left % 4 == 0 else left
-        left //= size
-        axes.append(("dp", left, size))
-    each = tuple((a,) for a in range(len(axes)))
-    return tuple(axes), each[::-1], each, each
+        return (("head", 2, 2), ("head", 1, 2), ("dp", 2, 4), ("dp", 1, 2)), (2, (0, 3), 1)
+    own = 2 if n_dp % 2 == 0 else 1
+    far = 4 if n_dp // own % 4 == 0 else 1
+    near = n_dp // own // far
+    return (("head", 1, n_head), ("dp", own * far, near), ("dp", own, far), ("dp", 1, own)), (2, (0, 1), 3)
 
 
 def digit(axis, stride, size):
@@ -570,30 +584,44 @@
 
 def greet(peers):
     barrier = pltpu.get_barrier_semaphore()
-    for device in peers:
+    for device, _, _ in peers:
         pl.semaphore_signal(barrier, inc=1, device_id=device, device_id_type=MESH)
     return lambda: pl.semaphore_wait(barrier, len(peers))
 
 
-def remote(src, dst, sems, n, device):
-    return pltpu.make_async_remote_copy(
-        src_ref=src,
-        dst_ref=dst,
-        send_sem=sems[0].at[n],
-        recv_sem=sems[1].at[n],
-        device_id=device,
-        device_id_type=MESH,
-    )
-
-
-def peers_of(axes, groups):
-    return [place for group in groups for place, _, _ in others(axes, group)]
-
-
-def gather_kernel(axes, groups, *refs):
+class Links:
+    def __init__(self, send, recv):
+        self.send, self.recv, self.count, self.started = send, recv, 0, []
+
+    def copy(self, n, src, dst, place):
+        return pltpu.make_async_remote_copy(
+            src_ref=src,
+            dst_ref=dst,
+            send_sem=self.send.at[n],
+            recv_sem=self.recv.at[n],
+            device_id=place,
+            device_id_type=MESH,
+        )
+
+    def start(self, src, dst, place, lands):
+        n = self.count
+        self.count += 1
+        out = self.copy(n, src, dst, place)
+        out.start()
+        self.started.append(out)
+        return self.copy(n, lands, lands, place).wait_recv
+
+    def drain(self):
+        for out in self.started:
+            out.wait_send()
+
+
+def gather_kernel(axes, roles, *refs):
     masters, w_ref = refs[:5], refs[5]
     held, (stage, block, local, send, recv) = refs[6:11], refs[11:]
-    arrived = greet(peers_of(axes, groups))
+    far, near, own = roles
+    line, plane, chip = others(axes, (far,)), others(axes, near), others(axes, (own,))
+    arrived = greet(line + plane + chip)
     loads = [pltpu.make_async_copy(m, h, local.at[n]) for n, (m, h) in enumerate(zip(masters, held))]
     for load in loads:
         load.start()
@@ -607,46 +635,36 @@
         stage[at : at + height, : part.shape[1]] = part[...]
         at += height
     block[...] = stage[...].astype(bf16)
-    have = [digit(*axis) for axis in axes]
-    keep = pltpu.make_async_copy(block, w_ref.at[tuple(have)], local.at[0])
+    mine = {a: digit(*axes[a]) for a in range(4)}
+    at = lambda digits: w_ref.at[tuple({**mine, **digits}[a] for a in range(4))]
+    keep = pltpu.make_async_copy(block, at({}), local.at[0])
     keep.start()
     arrived()
-    sent, n = [], 0
-    for group in groups:
-        coming = []
-        for place, _, source in others(axes, group):
-            mine = w_ref.at[tuple(have)]
-            copy = remote(block if n < len(others(axes, groups[0])) else mine, mine, (send, recv), n, place)
-            copy.start()
-            sent.append(copy)
-            there = list(have)
-            for a in group:
-                there[a] = source[a]
-            there = w_ref.at[tuple(there)]
-            coming.append(remote(there, there, (send, recv), n, place))
-            n += 1
-        if group is groups[0]:
-            keep.wait()
-        for copy in coming:
-            copy.wait_recv()
-        for a in group:
-            have[a] = slice(None)
-    for copy in sent:
-        copy.wait_send()
-
-
-def copies_of(axes, groups):
-    return sum(math.prod(axes[a][2] for a in group) - 1 for group in groups)
-
-
-def gather(axes, groups, rows, masters, cid=0, out=ANY):
-    copies = copies_of(axes, groups)
-    shape = tuple(size for _, _, size in axes) + (rows, 128)
+    links = Links(send, recv)
+    first = [links.start(block, at({}), place, at(source)) for place, _, source in line]
+
+    for wait in first:
+        wait()
+    keep.wait()
+    done = {far: slice(None)}
+    for group, peers in ((near, plane), ((own,), chip)):
+        block = at(done)
+        waits = [links.start(block, block, place, at({**done, **source})) for place, _, source in peers]
+        for wait in waits:
+            wait()
+        done.update({a: slice(None) for a in group})
+    links.drain()
+
+
+def gather(axes, roles, rows, masters, cid=0):
+    sizes = [size for _, _, size in axes]
+    far, near, own = roles
+    copies = sizes[far] + math.prod(sizes[a] for a in near) + sizes[own]
     return pl.pallas_call(
-        functools.partial(gather_kernel, axes, groups),
-        out_shape=jax.ShapeDtypeStruct(shape, bf16),
-        in_specs=[ANY] * 5,
-        out_specs=out,
+        functools.partial(gather_kernel, axes, roles),
+        out_shape=jax.ShapeDtypeStruct(tuple(sizes) + (rows, 128), bf16),
+        in_specs=[HBM] * 5,
+        out_specs=HBM,
         scratch_shapes=[pltpu.VMEM(m.shape, f32) for m in masters]
         + [
             pltpu.VMEM((rows, 128), f32),
@@ -661,96 +679,103 @@
     )(*masters)
 
 
-def scatter_kernel(axes, groups, sums, g_ref, red_ref, sq_ref, *scratch):
-    own, scratch = scratch[0], scratch[1:]
-    arrived, scratch = scratch[: len(groups)], scratch[len(groups) :]
-    partial, scratch = scratch[: len(groups) - 1], scratch[len(groups) - 1 :]
-    squares, (local, send, recv) = scratch[:-3], scratch[-3:]
-    peers = peers_of(axes, groups) + [p for s in sums if s not in groups for p in peers_of(axes, [s])]
-    ready = greet(peers)
-    left = list(range(len(axes)))
-    pick = lambda digits: tuple(digits.get(a, slice(None)) for a in left)
-    mine = lambda group: {a: digit(*axes[a]) for a in group}
-    load = pltpu.make_async_copy(g_ref.at[pick(mine(groups[0]))], own, local.at[0])
-    load.start()
+def scatter_kernel(axes, roles, g_ref, red_ref, sq_ref, *scratch):
+    held, from_chip, partial, from_plane, passed, from_line, sq_chip, sq_all, local, send, recv = scratch
+    far, near, own = roles
+    line, plane, chip = others(axes, (far,)), others(axes, near), others(axes, (own,))
+    every = others(axes, tuple(sorted((far,) + near)))
+    ready = greet(chip + every)
+    mine = {a: digit(*axes[a]) for a in range(4)}
+    pick = lambda digits: g_ref.at[tuple(digits.get(a, slice(None)) for a in range(4))]
+    pieces = [theirs for _, theirs, _ in line] + [{far: mine[far]}]
+    loads = []
+    for k, piece in enumerate(pieces):
+        loads.append(pltpu.make_async_copy(pick({**piece, own: mine[own]}), held.at[k], local.at[k]))
+        loads[-1].start()
     ready()
-    sent, n = [], 0
-    current = g_ref
-    for s, group in enumerate(groups):
-        coming = []
-        for o, (place, theirs, _) in enumerate(others(axes, group)):
-            copy = remote(current.at[pick(theirs)], arrived[s].at[o], (send, recv), n, place)
-            copy.start()
-            sent.append(copy)
-            coming.append(copy)
-            n += 1
-        if s == 0:
-            load.wait()
-            total = own[...].astype(f32)
-        else:
-            total = current[pick(mine(group))].astype(f32)
-        for o, copy in enumerate(coming):
-            copy.wait_recv()
-            total = total + arrived[s][o].astype(f32)
-        left = [a for a in left if a not in group]
-        if left:
-            partial[s][...] = total.astype(bf16)
-            current = partial[s]
+    links = Links(send, recv)
+    first = [
+        [
+            links.start(pick({**piece, **theirs}), from_chip.at[k, n], place, from_chip.at[k, n])
+            for n, (place, theirs, _) in enumerate(chip)
+        ]
+        for k, piece in enumerate(pieces)
+    ]
+    second = []
+    inner = lambda digits: tuple(digits[a] for a in near)
+    for k in range(len(pieces)):
+        loads[k].wait()
+        total = held[k].astype(f32)
+        for n, wait in enumerate(first[k]):
+            wait()
+            total = total + from_chip[k, n].astype(f32)
+        partial[k] = total.astype(bf16)
+        second.append(
+            [
+                links.start(partial.at[(k,) + inner(theirs)], from_plane.at[k, n], place, from_plane.at[k, n])
+                for n, (place, theirs, _) in enumerate(plane)
+            ]
+        )
+    third = []
+    for k in range(len(pieces)):
+        total = partial[(k,) + inner(mine)].astype(f32)
+        for n, wait in enumerate(second[k]):
+            wait()
+            total = total + from_plane[k, n].astype(f32)
+        if k < len(line):
+            passed[k] = total.astype(bf16)
+            third.append(links.start(passed.at[k], from_line.at[k], line[k][0], from_line.at[k]))
+    for n, wait in enumerate(third):
+        wait()
+        total = total + from_line[n].astype(f32)
     red_ref[...] = total
     square = total * total
     fold = square[0:8]
     for r in range(8, square.shape[0], 8):
         fold = fold + square[r : r + 8]
     fold = jnp.sum(fold, axis=0, keepdims=True)
-    for group, ref in zip(sums, squares):
-        digits = mine(group)
-        ref[tuple(digits[a] for a in group)] = fold
+    for group, peers, ref in (((own,), chip, sq_chip), (tuple(sorted((far,) + near)), every, sq_all)):
         at = lambda digits: ref.at[tuple(digits[a] for a in group)]
-        coming = []
-        for place, _, source in others(axes, group):
-            copy = remote(at(digits), at(digits), (send, recv), n, place)
-            copy.start()
-            sent.append(copy)
-            coming.append(remote(at(source), at(source), (send, recv), n, place))
-            n += 1
-        for copy in coming:
-            copy.wait_recv()
+        ref[tuple(mine[a] for a in group)] = fold
+        waits = [links.start(at(mine), at(mine), place, at(source)) for place, _, source in peers]
+        for wait in waits:
+            wait()
         fold = 0.0
         for index in itertools.product(*(range(axes[a][2]) for a in group)):
             fold = fold + ref[index]
     sq_ref[...] = fold
-    for copy in sent:
-        copy.wait_send()
-
-
-def scatter(axes, groups, sums, grads, cid=1):
-    size = lambda a: axes[a][2]
+    links.drain()
+
+
+def scatter(axes, roles, grads, cid=1):
+    sizes = [size for _, _, size in axes]
+    far, near, own = roles
     block = grads.shape[-2:]
-    left = list(range(len(axes)))
-    arrived, partial = [], []
-    for group in groups:
-        left = [a for a in left if a not in group]
-        shape = tuple(size(a) for a in left) + block
-        arrived.append(pltpu.VMEM((math.prod(size(a) for a in group) - 1,) + shape, bf16))
-        partial.append(pltpu.VMEM(shape, bf16))
-    squares = [pltpu.VMEM(tuple(size(a) for a in group) + (1, 128), f32) for group in sums]
-    copies = copies_of(axes, groups) + copies_of(axes, sums)
+    spread = tuple(sizes[a] for a in range(4) if a in near) + block
+    nf, np_, no = sizes[far], math.prod(sizes[a] for a in near), sizes[own]
+    least = lambda n: max(n, 1)
+    copies = nf * (no - 1) + nf * (np_ - 1) + (nf - 1) + (no - 1) + (nf * np_ - 1)
+    together = tuple(sizes[a] for a in sorted((far,) + near))
     return pl.pallas_call(
-        functools.partial(scatter_kernel, axes, groups, sums),
+        functools.partial(scatter_kernel, axes, roles),
         out_shape=(jax.ShapeDtypeStruct(block, f32), jax.ShapeDtypeStruct((1, 128), f32)),
-        in_specs=[ANY],
+        in_specs=[HBM],
         out_specs=(WHOLE, WHOLE),
-        scratch_shapes=[partial[0]]
-        + arrived
-        + partial[:-1]
-        + squares
-        + [
-            pltpu.SemaphoreType.DMA((1,)),
+        scratch_shapes=[
+            pltpu.VMEM((nf,) + spread, bf16),
+            pltpu.VMEM((nf, least(no - 1)) + spread, bf16),
+            pltpu.VMEM((nf,) + spread, bf16),
+            pltpu.VMEM((nf, least(np_ - 1)) + block, bf16),
+            pltpu.VMEM((least(nf - 1),) + block, bf16),
+            pltpu.VMEM((least(nf - 1),) + block, bf16),
+            pltpu.VMEM((no, 1, 128), f32),
+            pltpu.VMEM(together + (1, 128), f32),
+            pltpu.SemaphoreType.DMA((nf,)),
             pltpu.SemaphoreType.DMA((copies,)),
             pltpu.SemaphoreType.DMA((copies,)),
         ],
         compiler_params=pltpu.CompilerParams(
-            collective_id=cid, has_side_effects=True, vmem_limit_bytes=65228 * 1024
+            collective_id=cid, has_side_effects=True, vmem_limit_bytes=62 * 1024 * 1024
         ),
     )(grads)
 
@@ -767,8 +792,14 @@
     return weight - rate * (direction + decay * weight), first_new, second_new
 
 
-def update_kernel(red, sq, *refs):
-    params, outs = refs[:15], refs[15:]
+def update_kernel(*refs):
+    held = refs[-18:-1]
+    copies = [pltpu.make_async_copy(src, dst, refs[-1].at[n]) for n, (src, dst) in enumerate(zip(refs, held))]
+    for copy in copies:
+        copy.start()
+    for copy in copies:
+        copy.wait()
+    (red, sq, *params), outs = held, refs[17:-18]
     rd, ro = params[0].shape[0], params[1].shape[0]
     norm = jnp.sqrt(jnp.sum(sq[...], keepdims=True))
     outs[0][...] = norm
@@ -798,9 +829,10 @@
     return pl.pallas_call(
         update_kernel,
         out_shape=shapes,
-        in_specs=[WHOLE] * 17,
+        in_specs=[HBM] * 17,
         out_specs=[WHOLE] * len(shapes),
-        compiler_params=pltpu.CompilerParams(vmem_limit_bytes=32 * 1024 * 1024),
+        scratch_shapes=[pltpu.VMEM(a.shape, f32) for a in (red, sq, *params)] + [pltpu.SemaphoreType.DMA((17,))],
+        compiler_params=pltpu.CompilerParams(vmem_limit_bytes=62 * 1024 * 1024),
     )(red, sq, *params)
 
 
@@ -808,11 +840,11 @@
     masters = params[:5]
     rd, ro = masters[0].shape[0], masters[1].shape[0]
     rows = -(-(3 * rd + 2 * ro) // 16) * 16
-    axes, inward, outward, sums = factors(n_dp, n_head)
-    weights = gather(axes, inward, rows, masters).reshape(n_head, n_dp, rows, 128)
+    axes, roles = factors(n_dp, n_head)
+    weights = gather(axes, roles, rows, masters).reshape(n_head, n_dp, rows, 128)
     mixed, input_grad, grads = layer(lengths, weights, tokens, cotangent, rd, ro)
     grads = grads.reshape(tuple(size for _, _, size in axes) + (rows, 128))
-    red, sq = scatter(axes, outward, sums, grads)
+    red, sq = scatter(axes, roles, grads)
     outs = update(red, sq, params)
     return (mixed, input_grad, outs[0].reshape(()), *outs[1:])
 

time: 103 us -> 96 us (0.932)
  Pallas kernels: 99.9 us -> 95.1 us
  local copies, waits for them, and re-layouts: 1.38 us -> 0 us
    pallas_call x1, Pallas kernels: 63 us -> 56.6 us  [layer(): pl.pallas_call(functools.partial(layer_kernel, rd, ro), out_shape=(jax.Sh...]
    pallas_call x3, Pallas kernels: 36.8 us -> 38.4 us  [the longest x1 21.2 us: scatter(): pl.pallas_call(functools.partial(scatter_kernel, axes, roles), out_shape=...]
    unnamed x34 -> x0, local copies, waits for them, and re-layouts: 1.38 us -> none
where the time goes in v4:
time: 96 us; the launch traced here: 95.8 us
  Pallas kernels  95.1 us (99%)
    pallas_call x1, Pallas kernels, layer(): pl.pallas_call(functools.partial(layer_kernel, rd, ro), out_shape=(jax.Sh...  56.6 us
    pallas_call x1, Pallas kernels, scatter(): pl.pallas_call(functools.partial(scatter_kernel, axes, roles), out_shape=...  21.2 us
    pallas_call x1, Pallas kernels, gather(): pl.pallas_call(functools.partial(gather_kernel, axes, roles), out_shape=j...  15.3 us
    pallas_call x1, Pallas kernels, update(): pl.pallas_call(update_kernel, out_shape=shapes, in_specs=[HBM] * 17, out_...  1.93 us

profile of v4, /device:TPU:0, one launch (start us, length us, event | category | flops | bytes accessed | tf_op | source)
XLA Modules:
  0.0 95.8 jit_solution(8302004992363320050)
XLA Ops:
  0.7 15.3 %shard_map.393 = bf16[2,2,4,2,64,128]{5,4,3,2,1,0:T(8,128)(2,1)} custom-call(f32[16,96]{1,0:T(8,128)} %refs_2_.3, f32[4,128]{1,0:T(4,128)} %refs_3_.3, f32[16,128]{1,0:T(8,128)} %refs_4_.3, f32[16,128]{1,0:T(8,128)} %refs_5_.1, f32[4,4]{1,0:T(4,128)} %refs_6_.1), custom_call_target="tpu_custom_call" | custom-call | tf_op jit(solution)/shard_map/pallas_call | solution.py:663
  16.0 56.6 %shard_map.394 = (bf16[4096,128]{1,0:T(8,128)(2,1)}, bf16[4096,128]{1,0:T(8,128)(2,1)}, bf16[4,8,64,128]{3,2,1,0:T(8,128)(2,1)}) custom-call(s32[4,8]{1,0:T(4,128)} %lengths.1, bf16[4,8,64,128]{3,2,1,0:T(8,128)(2,1)} %bitcast.3, bf16[4096,128]{1,0:T(8,128)(2,1)} %tokens_hbm.1, bf16[4096,128]{1,0:T(8,128)(2,1)} %cot_hbm.1), custom_call_target="tpu_custom_call" | custom-call | tf_op jit(solution)/shard_map/pallas_call | solution.py:542
  72.6 21.2 %shard_map.395 = (f32[64,128]{1,0:T(8,128)}, f32[1,128]{1,0:T(1,128)}) custom-call(bf16[2,2,4,2,64,128]{5,4,3,2,1,0:T(8,128)(2,1)} %bitcast.4), custom_call_target="tpu_custom_call" | custom-call | tf_op jit(solution)/shard_map/pallas_call | solution.py:759
  93.8 1.9 %shard_map.396 = (f32[1,1]{1,0:T(1,128)}, f32[16,96]{1,0:T(8,128)}, f32[16,96]{1,0:T(8,128)}, f32[16,96]{1,0:T(8,128)}, f32[4,128]{1,0:T(4,128)}, /*index=5*/f32...) custom-call(f32[64,128]{1,0:T(8,128)} %get-tuple-element.62.refs_0_,, ...), custom_call_target="tpu_custom_call" | custom-call | tf_op jit(solution)/shard_map/pallas_call | solution.py:829
